TPU v7x, 512 devices: a whole 4x4x16 slice. The times are simulated.
512 devices in a mesh: line: 8 (over x, core), chip: 16 (over z), layer: 4 (over y).
Axes of the slice: x: 4, y: 4, z: 16, core: 2. Of those that a mesh axis runs over, the one named last changes fastest.
Arguments:
- warmth_field: float32 [512, 64, 2048], P('line', 'layer', 'chip'), may hold values from -1.5 to 1.5
- power_input: float32 [512, 64, 2048], P('line', 'layer', 'chip'), may hold values from -24 to 24
- inertia_weight: float32 [512, 64, 2048], P('line', 'layer', 'chip'), may hold values from 0.0012207031 to 0.0048828125
- conductivity_lookup: float32 [8], replicated, may hold values from 2 to 40
- substance_label: int32 [512, 64, 2048], P('line', 'layer', 'chip'), may hold values from 0 to 7
Outputs:
- residual: float32 [512, 64, 2048], P('line', 'layer', 'chip')
- heat_rate: float32 [512, 64, 2048], P('line', 'layer', 'chip')
All inputs are finite; a program needn't handle non-finite values.
Results may differ from a plain program's by a relative error of at most 0.0037.
Values sent between devices are 32-bit elements; how exact they have to be, the bound alone decides.
A program may use at most 64 MiB of HBM per device.

v0:
```python
import jax
import jax.numpy as jnp
from jax import lax
from jax.sharding import PartitionSpec as P


def with_halo(cells, sides, width):
    for axis, dim in sides:
        count = lax.axis_size(axis)
        ends = count - 1
        head = lax.slice_in_dim(cells, 0, width, axis=dim)
        tail = lax.slice_in_dim(cells, cells.shape[dim] - width, cells.shape[dim], axis=dim)
        cells = jnp.concatenate(
            [
                lax.ppermute(tail, axis, [(i, (i + 1) % count) for i in range(ends)]),
                cells,
                lax.ppermute(head, axis, [((i + 1) % count, i) for i in range(ends)]),
            ],
            axis=dim,
        )
    return cells


def conductance(first, second):
    return 2.0 * first * second / jnp.maximum(first + second, 1e-30)


def compose(left, right):
    denom = 1.0 - left[5] * right[1]
    mid_const = (left[3] + left[5] * right[0]) / denom
    mid_left = left[4] / denom
    mid_right = left[5] * right[2] / denom
    next_const = right[0] + right[1] * mid_const
    next_left = right[1] * mid_left
    next_right = right[1] * mid_right + right[2]
    return (
        left[0] + left[2] * next_const,
        left[1] + left[2] * next_left,
        left[2] * next_right,
        right[3] + right[4] * mid_const,
        right[4] * mid_left,
        right[4] * mid_right + right[5],
    )


def shards(warmth_field, power_input, inertia_weight, conductivity_lookup, substance_label):
    coupling_strength = jnp.zeros(warmth_field.shape, jnp.float32)
    for mat_id in range(conductivity_lookup.shape[0]):
        coupling_strength = coupling_strength + jnp.where(
            substance_label == mat_id, conductivity_lookup[mat_id], 0.0
        )
    piled_tiers = jnp.stack([warmth_field, coupling_strength])
    bordered_array = with_halo(piled_tiers, (("line", 1), ("chip", 3), ("layer", 2)), 1)
    bordered_warmth = bordered_array[0]
    cond_pad = bordered_array[1]
    shifts = [
        (slice(2, None), slice(1, -1), slice(1, -1)),
        (slice(None, -2), slice(1, -1), slice(1, -1)),
        (slice(1, -1), slice(2, None), slice(1, -1)),
        (slice(1, -1), slice(None, -2), slice(1, -1)),
        (slice(1, -1), slice(1, -1), slice(2, None)),
        (slice(1, -1), slice(1, -1), slice(None, -2)),
    ]
    energy_current = jnp.zeros_like(warmth_field)
    faces = []
    for choose_by_predicate in shifts:
        interface_average = conductance(coupling_strength, cond_pad[choose_by_predicate])
        faces.append(interface_average)
        energy_current = energy_current + interface_average * (
            warmth_field - bordered_warmth[choose_by_predicate]
        )
    tier_total = warmth_field.shape[1]
    is_last = lax.axis_index("layer") == lax.axis_size("layer") - 1
    topmost_boundary_flag = jnp.logical_and(
        lax.broadcasted_iota(jnp.int32, (1, tier_total, 1), 1) == tier_total - 1, is_last
    )
    energy_current = energy_current + jnp.where(
        topmost_boundary_flag, coupling_strength * warmth_field, 0.0
    )
    residual = power_input - energy_current
    rhs = lax.optimization_barrier(residual.astype(jnp.bfloat16)).astype(jnp.float32)
    gplus = faces[0]
    gminus = faces[1]
    lower = -gminus
    upper = -gplus
    diag = inertia_weight + gminus + gplus
    empty = jnp.zeros_like(rhs)
    spike_left = empty.at[0].set(lower[0])
    spike_right = empty.at[-1].set(upper[-1])
    rights = jnp.stack([rhs, spike_left, spike_right], axis=1)
    inner_low = lower.at[0].set(0.0)
    inner_up = upper.at[-1].set(0.0)

    def forward(carry, row):
        prev_c, prev_d = carry
        low, up, dia, right = row
        denom = dia - low * prev_c
        new_c = up / denom
        new_d = (right - low[None] * prev_d) / denom[None]
        return ((new_c, new_d), (new_c, new_d))

    lateral_sheet = jnp.zeros(warmth_field.shape[1:], jnp.float32)
    _, (coef_c, coef_d) = lax.scan(
        forward,
        (lateral_sheet, jnp.zeros(rights.shape[1:], jnp.float32)),
        (inner_low, inner_up, diag, rights),
        unroll=True,
    )

    def backward(after, row):
        cc, dd = row
        value = dd - cc[None] * after
        return (value, value)

    _, solved = lax.scan(
        backward,
        jnp.zeros(rights.shape[1:], jnp.float32),
        (coef_c, coef_d),
        reverse=True,
        unroll=True,
    )
    local_sol = solved[:, 0]
    left_spike = solved[:, 1]
    right_spike = solved[:, 2]
    relation = (
        local_sol[0],
        -left_spike[0],
        -right_spike[0],
        local_sol[-1],
        -left_spike[-1],
        -right_spike[-1],
    )
    ident = (
        lateral_sheet,
        lateral_sheet,
        lateral_sheet + 1.0,
        lateral_sheet,
        lateral_sheet + 1.0,
        lateral_sheet,
    )
    packed = jnp.stack(relation)[None]
    every = lax.all_gather(packed, "line", axis=0, tiled=True)
    count = every.shape[0]
    mine = lax.axis_index("line")

    def prefix_step(index, carry):
        entry = tuple((every[index, slot] for slot in range(6)))
        joined = compose(carry, entry)
        return jax.tree.map(lambda new, old: jnp.where(index < mine, new, old), joined, carry)

    def suffix_step(index, carry):
        other = count - 1 - index
        entry = tuple((every[other, slot] for slot in range(6)))
        joined = compose(entry, carry)
        return jax.tree.map(lambda new, old: jnp.where(other > mine, new, old), joined, carry)

    before = lax.fori_loop(0, count, prefix_step, ident)
    after_rel = lax.fori_loop(0, count, suffix_step, ident)
    top_left = 1.0 + left_spike[0] * before[5]
    top_right = right_spike[0] * after_rel[1]
    low_left = left_spike[-1] * before[5]
    low_right = 1.0 + right_spike[-1] * after_rel[1]
    first_rhs = local_sol[0] - left_spike[0] * before[3] - right_spike[0] * after_rel[0]
    last_rhs = local_sol[-1] - left_spike[-1] * before[3] - right_spike[-1] * after_rel[0]
    determ = top_left * low_right - top_right * low_left
    first_val = (first_rhs * low_right - top_right * last_rhs) / determ
    last_val = (top_left * last_rhs - low_left * first_rhs) / determ
    left_val = before[3] + before[5] * first_val
    right_val = after_rel[0] + after_rel[1] * last_val
    correction = local_sol - left_spike * left_val[None] - right_spike * right_val[None]
    return (residual, inertia_weight * correction)


def solution(mesh):
    return jax.shard_map(
        shards,
        mesh=mesh,
        in_specs=(
            P("line", "layer", "chip"),
            P("line", "layer", "chip"),
            P("line", "layer", "chip"),
            P(),
            P("line", "layer", "chip"),
        ),
        out_specs=(P("line", "layer", "chip"), P("line", "layer", "chip")),
        check_vma=False,
    )
```

profile of v0, /device:TPU:1, one launch (start us, length us, event | category | flops | bytes accessed | tf_op | source)
XLA Modules:
  0.0 141.7 jit_solution(3498176266723342964)
XLA Ops:
  0.6 1.6 %fusion.354 = (f32[1]{0:T(128)}, f32[1]{0:T(128)}, f32[1]{0:T(128)}, f32[1]{0:T(128)}, f32[1]{0:T(128)}, /*index=5*/f32[1]{0:T(128)}, f32[1]{0:T(128)}, f32[1]{0:T(128)}) fusion(f32[8]{0:T(128)} %param.20), kind=kLoop, calls=%fused_computation.798 | loop fusion | bytes 64 | tf_op jit(solution)/shard_map/slice | solution.py:50
  2.3 6.4 %fusion.298 = f32[1,64,16,128]{3,2,1,0:T(8,128)S(1)} fusion(f32[]{:T(128)} %bitcast.7, s32[64,16,128]{2,1,0:T(8,128)} %param.21, f32[]{:T(128)} %bitcast.6, f32[]{:T(128)} %bitcast.5, f32[]{:T(128)} %bitcast.4, f32[]{:T(128)} %bitcast.3, f32[]{:T(128)} %bitcast.2, f32[]{:T(128)} %bitcast.1, f32[]{:T(128)} %bitcast), kind=kLoop, calls=%fused_computation.795 | loop fusion | flops 3014656 | bytes 1048608 | tf_op jit(solution)/shard_map/stack | solution.py:52
  8.6 0.7 pad_maximum_fusion.9
  9.3 4.5 %collective-permute-start = (f32[2,1,16,128]{3,2,1,0:T(8,128)S(1)}, f32[2,1,16,128]{3,2,1,0:T(8,128)S(1)}, u32[]{:S(2)}, u32[]{:S(2)}) collective-permute-start(f32[2,1,16,128]{3,2,1,0:T(8,128)S(1)} %get-tuple-element.558), channel_id=1, source_target_pairs={{0,64},{64,128},{128,192},{192,256},{256,320},{320,384},{384,448},... | collective-permute-start | bytes 49160 | tf_op jit(solution)/shard_map/ppermute | solution.py:15
  13.9 5.6 %collective-permute-start.1 = (f32[2,1,16,128]{3,2,1,0:T(8,128)S(1)}, f32[2,1,16,128]{3,2,1,0:T(8,128)S(1)}, u32[]{:S(2)}, u32[]{:S(2)}) collective-permute-start(f32[2,1,16,128]{3,2,1,0:T(8,128)S(1)} %get-tuple-element.559), channel_id=1, source_target_pairs={{64,0},{128,64},{192,128},{256,192},{320,256},{384,320},{448,384},... | collective-permute-start | bytes 49160 | tf_op jit(solution)/shard_map/ppermute | solution.py:17
  19.4 0.8 collective-permute-done.1
  21.2 2.2 %collective-permute-start.2 = (f32[2,66,16,1]{1,2,3,0:T(8,128)S(1)}, f32[2,66,16,1]{1,2,3,0:T(8,128)S(1)}, u32[]{:S(2)}, u32[]{:S(2)}) collective-permute-start(f32[2,66,16,1]{1,2,3,0:T(8,128)S(1)} %copy.278), channel_id=1, source_target_pairs={{0,4},{4,8},{8,12},{12,16},{16,20},{20,24},{24,28},{28,32},{32,36}... | collective-permute-start | bytes 25352 | tf_op jit(solution)/shard_map/ppermute | solution.py:15
  23.9 1.3 collective-permute-start.3
  25.8 2.7 %collective-permute-done.3 = f32[2,66,16,1]{1,2,3,0:T(8,128)S(1)} collective-permute-done((f32[2,66,16,1]{1,2,3,0:T(8,128)S(1)}, f32[2,66,16,1]{1,2,3,0:T(8,128)S(1)}, u32[]{:S(2)}, u32[]{:S(2)}) %collective-permute-start.3) | collective-permute-done | bytes 8480 | tf_op jit(solution)/shard_map/ppermute | solution.py:17
  29.2 0.9 pad_maximum_fusion.7
  30.1 3.2 %collective-permute-start.4 = (f32[2,66,1,130]{3,2,1,0:T(1,128)S(1)}, f32[2,66,1,130]{3,2,1,0:T(1,128)S(1)}, u32[]{:S(2)}, u32[]{:S(2)}) collective-permute-start(f32[2,66,1,130]{3,2,1,0:T(1,128)S(1)} %get-tuple-element.550), channel_id=1, source_target_pairs={{0,1},{1,2},{2,3},{4,5},{5,6},{6,7},{8,9},{9,10},{10,11},{12,13},{... | collective-permute-start | bytes 205928 | tf_op jit(solution)/shard_map/ppermute | solution.py:15
  33.3 1.3 collective-permute-start.5
  34.6 1.8 %collective-permute-done.4 = f32[2,66,1,130]{3,2,1,0:T(1,128)S(1)} collective-permute-done((f32[2,66,1,130]{3,2,1,0:T(1,128)S(1)}, f32[2,66,1,130]{3,2,1,0:T(1,128)S(1)}, u32[]{:S(2)}, u32[]{:S(2)}) %collective-permute-start.4) | collective-permute-done | bytes 68672 | tf_op jit(solution)/shard_map/ppermute | solution.py:15
  36.4 4.4 %collective-permute-done.5 = f32[2,66,1,130]{3,2,1,0:T(1,128)S(1)} collective-permute-done((f32[2,66,1,130]{3,2,1,0:T(1,128)S(1)}, f32[2,66,1,130]{3,2,1,0:T(1,128)S(1)}, u32[]{:S(2)}, u32[]{:S(2)}) %collective-permute-start.5) | collective-permute-done | bytes 68672 | tf_op jit(solution)/shard_map/ppermute | solution.py:17
  40.8 2.9 %pad_maximum_fusion = f32[2,66,18,130]{3,2,1,0:T(8,128)S(1)} fusion(f32[2,66,1,130]{3,2,1,0:T(1,128)S(1)} %collective-permute-done.5, f32[2,66,16,1]{3,2,1,0:T(8,128)S(1)} %copy.281, f32[2,1,16,128]{3,2,1,0:T(8,128)S(1)} %collective-permute-done.1, f32[1,64,16,128]{3,2,1,0:T(8,128)S(1)} %fusion.298, f32[1,64,16,128]{3,2,1,0:T(8,128)S(1)} %bitcast.2145, ...), kind=kLoop, calls=%fused_computation.28 | loop fusion | flops 2162160 | bytes 2471040 | tf_op jit(solution)/shard_map/concatenate | solution.py:13
  43.9 0.8 copy-done.1
  44.8 5.7 %add_add_fusion = (f32[64,16,128]{2,1,0:T(8,128)S(1)}, f32[64,16,128]{2,1,0:T(8,128)S(1)}, f32[64,16,128]{2,1,0:T(8,128)S(1)}) fusion(f32[64,16,128]{2,1,0:T(8,128)S(1)} %copy-done.2, f32[66,18,130]{2,1,0:T(8,128)S(1)} %get-tuple-element.548, f32[]{:T(128)} %bitcast.7, s32[64,16,128]{2,1,0:T(8,128)S(1)} %copy-done.1, f32[]{:T(128)} %bitcast.6, f32[]{:T(128)} %bitcast.5, ...), kind=kLoop, calls=%fused_computation.65 | loop fusion | flops 4718592 | bytes 3670048 | tf_op jit(solution)/shard_map/add | solution.py:86
  50.9 0.6 fusion.254
  51.6 0.6 fusion.141
  52.2 0.6 fusion.137
  53.4 0.6 fusion.129
  54.0 0.6 fusion.125
  54.7 0.6 fusion.121
  55.3 0.6 fusion.117
  55.9 0.6 fusion.113
  56.5 0.6 fusion.109
  57.1 0.6 divide_multiply_fusion
  57.8 0.6 fusion.255
  58.4 0.6 fusion.256
  59.1 0.6 fusion.259
  59.7 0.6 fusion.261
  60.4 0.6 fusion.263
  61.0 0.6 fusion.265
  61.6 0.6 fusion.267
  62.3 0.6 fusion.269
  63.6 0.6 fusion.273
  64.2 0.6 fusion.275
  64.9 0.6 fusion.277
  66.1 0.6 fusion.281
  66.8 0.6 fusion.283
  67.4 0.6 fusion.285
  68.1 0.6 fusion.287
  68.7 0.6 fusion.289
  69.3 0.6 fusion.291
  71.2 0.7 divide_bitcast_fusion
  71.9 7.8 %fusion.351 = (bf16[64,16,128]{2,1,0:T(8,128)(2,1)S(1)}, f32[64,16,128]{2,1,0:T(8,128)}) fusion(f32[64,16,128]{2,1,0:T(8,128)S(1)} %copy-done.3, f32[64,16,128]{2,1,0:T(8,128)S(1)} %copy-done, pred[16]{0:T(512)(128)(4,1)S(1)} %compare_and_fusion, f32[66,18,130]{2,1,0:T(8,128)S(1)} %get-tuple-element.549, f32[66,18,130]{2,1,0:T(8,128)S(1)} %get-tuple-element.548, ...), kind=kLoop, calls=%fused_computation.796 | loop fusion | flops 9175040 | bytes 8650800 | tf_op jit(solution)/shard_map/convert_element_type | solution.py:81
  79.9 1.2 fusion.65
  81.4 2.4 %constant_dynamic-update-slice_fusion.63 = (f32[64,3,16,128]{3,2,1,0:T(8,128)}, f32[1,3,16,128]{3,2,1,0:T(8,128)S(1)}, f32[3,16,128]{2,1,0:T(8,128)}, f32[3,16,1...) fusion(f32[3,16,128]{2,1,0:T(8,128)S(1)} %get-tuple-element.541, ...), kind=kLoop, calls=%fused_computation.139 | loop fusion | flops 1744895 | bytes 3522560
  83.9 13.5 %all-gather = f32[48,16,128]{2,1,0:T(8,128)S(1)} all-gather(f32[6,16,128]{2,1,0:T(8,128)S(1)} %constant_dynamic-update-slice_fusion.64), channel_id=2, replica_groups=mesh['line'=8,'chip'=16,'layer'=4] {'line'}, dimensions={0}, use_global_device_ids=true | all-gather | bytes 442368 | tf_op jit(solution)/shard_map/all_gather | solution.py:142
  98.3 3.2 %constant_dynamic-update-slice_fusion.62 = (f32[64,3,16,128]{3,2,1,0:T(8,128)}, f32[1,3,16,128]{3,2,1,0:T(8,128)S(1)}, f32[1,3,16,128]{3,2,1,0:T(8,128)S(1)}, f3...) fusion(f32[64,3,16,128]{3,2,1,0:T(8,128)} %get-tuple-element.38, ...), kind=kLoop, calls=%fused_computation.138 | loop fusion | flops 1935360 | bytes 4161536
  103.4 0.6 constant_dynamic-update-slice_fusion.58
  105.9 0.6 constant_dynamic-update-slice_fusion.54
  108.9 0.6 constant_dynamic-update-slice_fusion.49
  111.4 0.6 constant_dynamic-update-slice_fusion.45
  112.0 0.6 constant_dynamic-update-slice_fusion.44
  118.1 0.6 constant_dynamic-update-slice_fusion.34
  121.1 0.6 constant_dynamic-update-slice_fusion.29
  123.5 0.6 constant_dynamic-update-slice_fusion.25
  125.3 0.6 constant_dynamic-update-slice_fusion.22
  130.8 0.6 constant_dynamic-update-slice_fusion.13
  133.2 0.6 constant_dynamic-update-slice_fusion.9
  135.7 0.6 constant_dynamic-update-slice_fusion.5
  138.1 0.6 constant_dynamic-update-slice_fusion.1
  139.3 2.3 %fusion.24 = f32[64,16,128]{2,1,0:T(8,128)} fusion(f32[64,16,128]{2,1,0:T(8,128)S(1)} %copy-done.2, f32[64,3,16,128]{3,2,1,0:T(8,128)} %constant_dynamic-update-slice_fusion, f32[16,128]{1,0:T(8,128)S(1)} %get-tuple-element.627, f32[16,128]{1,0:T(8,128)S(1)} %get-tuple-element.626), kind=kLoop, calls=%fused_computation.41 | loop fusion | flops 655360 | bytes 2637824 | tf_op jit(solution)/shard_map/mul | solution.py:171
  (254 shorter events, 37.8 us)
Async XLA Ops:
  0.6 19.6 %copy-start = (f32[64,16,128]{2,1,0:T(8,128)S(1)}, f32[64,16,128]{2,1,0:T(8,128)}, u32[]{:S(2)}) copy-start(f32[64,16,128]{2,1,0:T(8,128)} %param.17) | copy-start | bytes 1572868
  9.3 10.1 %collective-permute-start = (f32[2,1,16,128]{3,2,1,0:T(8,128)S(1)}, f32[2,1,16,128]{3,2,1,0:T(8,128)S(1)}, u32[]{:S(2)}, u32[]{:S(2)}) collective-permute-start(f32[2,1,16,128]{3,2,1,0:T(8,128)S(1)} %get-tuple-element.558), channel_id=1, source_target_pairs={{0,64},{64,128},{128,192},{192,256},{256,320},{320,384},{384,448},... | collective-permute-start | bytes 49160 | tf_op jit(solution)/shard_map/ppermute | solution.py:15
  13.9 6.4 %collective-permute-start.1 = (f32[2,1,16,128]{3,2,1,0:T(8,128)S(1)}, f32[2,1,16,128]{3,2,1,0:T(8,128)S(1)}, u32[]{:S(2)}, u32[]{:S(2)}) collective-permute-start(f32[2,1,16,128]{3,2,1,0:T(8,128)S(1)} %get-tuple-element.559), channel_id=1, source_target_pairs={{64,0},{128,64},{192,128},{256,192},{320,256},{384,320},{448,384},... | collective-permute-start | bytes 49160 | tf_op jit(solution)/shard_map/ppermute | solution.py:17
  21.2 4.1 %collective-permute-start.2 = (f32[2,66,16,1]{1,2,3,0:T(8,128)S(1)}, f32[2,66,16,1]{1,2,3,0:T(8,128)S(1)}, u32[]{:S(2)}, u32[]{:S(2)}) collective-permute-start(f32[2,66,16,1]{1,2,3,0:T(8,128)S(1)} %copy.278), channel_id=1, source_target_pairs={{0,4},{4,8},{8,12},{12,16},{16,20},{20,24},{24,28},{28,32},{32,36}... | collective-permute-start | bytes 25352 | tf_op jit(solution)/shard_map/ppermute | solution.py:15
  23.9 4.7 %collective-permute-start.3 = (f32[2,66,16,1]{1,2,3,0:T(8,128)S(1)}, f32[2,66,16,1]{1,2,3,0:T(8,128)S(1)}, u32[]{:S(2)}, u32[]{:S(2)}) collective-permute-start(f32[2,66,16,1]{1,2,3,0:T(8,128)S(1)} %copy.279), channel_id=1, source_target_pairs={{4,0},{8,4},{12,8},{16,12},{20,16},{24,20},{28,24},{32,28},{36,32}... | collective-permute-start | bytes 25352 | tf_op jit(solution)/shard_map/ppermute | solution.py:17
  30.1 6.3 %collective-permute-start.4 = (f32[2,66,1,130]{3,2,1,0:T(1,128)S(1)}, f32[2,66,1,130]{3,2,1,0:T(1,128)S(1)}, u32[]{:S(2)}, u32[]{:S(2)}) collective-permute-start(f32[2,66,1,130]{3,2,1,0:T(1,128)S(1)} %get-tuple-element.550), channel_id=1, source_target_pairs={{0,1},{1,2},{2,3},{4,5},{5,6},{6,7},{8,9},{9,10},{10,11},{12,13},{... | collective-permute-start | bytes 205928 | tf_op jit(solution)/shard_map/ppermute | solution.py:15
  33.3 7.5 %collective-permute-start.5 = (f32[2,66,1,130]{3,2,1,0:T(1,128)S(1)}, f32[2,66,1,130]{3,2,1,0:T(1,128)S(1)}, u32[]{:S(2)}, u32[]{:S(2)}) collective-permute-start(f32[2,66,1,130]{3,2,1,0:T(1,128)S(1)} %get-tuple-element.551), channel_id=1, source_target_pairs={{1,0},{2,1},{3,2},{5,4},{6,5},{7,6},{9,8},{10,9},{11,10},{13,12},{... | collective-permute-start | bytes 205928 | tf_op jit(solution)/shard_map/ppermute | solution.py:17
  50.9 28.9 %copy-start.66 = (f32[16,128]{1,0:T(8,128)}, f32[16,128]{1,0:T(8,128)S(1)}, u32[]{:S(2)}) copy-start(f32[16,128]{1,0:T(8,128)S(1)} %get-tuple-element.492) | copy-start | bytes 24580
  50.9 30.2 %copy-start.65 = (f32[16,128]{1,0:T(8,128)}, f32[16,128]{1,0:T(8,128)S(1)}, u32[]{:S(2)}) copy-start(f32[16,128]{1,0:T(8,128)S(1)} %get-tuple-element.491) | copy-start | bytes 24580
  51.6 29.6 %copy-start.69 = (f32[16,128]{1,0:T(8,128)}, f32[16,128]{1,0:T(8,128)S(1)}, u32[]{:S(2)}) copy-start(f32[16,128]{1,0:T(8,128)S(1)} %get-tuple-element.405) | copy-start | bytes 24580
  52.2 28.9 %copy-start.34 = (f32[16,128]{1,0:T(8,128)}, f32[16,128]{1,0:T(8,128)S(1)}, u32[]{:S(2)}) copy-start(f32[16,128]{1,0:T(8,128)S(1)} %get-tuple-element.494) | copy-start | bytes 24580
  52.8 28.3 %copy-start.35 = (f32[16,128]{1,0:T(8,128)}, f32[16,128]{1,0:T(8,128)S(1)}, u32[]{:S(2)}) copy-start(f32[16,128]{1,0:T(8,128)S(1)} %get-tuple-element.498) | copy-start | bytes 24580
  53.4 27.7 %copy-start.36 = (f32[16,128]{1,0:T(8,128)}, f32[16,128]{1,0:T(8,128)S(1)}, u32[]{:S(2)}) copy-start(f32[16,128]{1,0:T(8,128)S(1)} %get-tuple-element.502) | copy-start | bytes 24580
  54.0 27.1 %copy-start.37 = (f32[16,128]{1,0:T(8,128)}, f32[16,128]{1,0:T(8,128)S(1)}, u32[]{:S(2)}) copy-start(f32[16,128]{1,0:T(8,128)S(1)} %get-tuple-element.506) | copy-start | bytes 24580
  54.7 26.5 %copy-start.38 = (f32[16,128]{1,0:T(8,128)}, f32[16,128]{1,0:T(8,128)S(1)}, u32[]{:S(2)}) copy-start(f32[16,128]{1,0:T(8,128)S(1)} %get-tuple-element.510) | copy-start | bytes 24580
  55.3 25.9 %copy-start.39 = (f32[16,128]{1,0:T(8,128)}, f32[16,128]{1,0:T(8,128)S(1)}, u32[]{:S(2)}) copy-start(f32[16,128]{1,0:T(8,128)S(1)} %get-tuple-element.514) | copy-start | bytes 24580
  55.9 25.3 %copy-start.40 = (f32[16,128]{1,0:T(8,128)}, f32[16,128]{1,0:T(8,128)S(1)}, u32[]{:S(2)}) copy-start(f32[16,128]{1,0:T(8,128)S(1)} %get-tuple-element.518) | copy-start | bytes 24580
  56.5 24.7 %copy-start.41 = (f32[16,128]{1,0:T(8,128)}, f32[16,128]{1,0:T(8,128)S(1)}, u32[]{:S(2)}) copy-start(f32[16,128]{1,0:T(8,128)S(1)} %get-tuple-element.522) | copy-start | bytes 24580
  57.1 24.1 %copy-start.51 = (f32[16,128]{1,0:T(8,128)}, f32[16,128]{1,0:T(8,128)S(1)}, u32[]{:S(2)}) copy-start(f32[16,128]{1,0:T(8,128)S(1)} %get-tuple-element.526) | copy-start | bytes 24580
  58.4 13.5 %copy-start.3 = (f32[64,16,128]{2,1,0:T(8,128)S(1)}, f32[64,16,128]{2,1,0:T(8,128)}, u32[]{:S(2)}) copy-start(f32[64,16,128]{2,1,0:T(8,128)} %param.18) | copy-start | bytes 1572868
  59.0 22.2 %copy-start.12 = (f32[16,128]{1,0:T(8,128)}, f32[16,128]{1,0:T(8,128)S(1)}, u32[]{:S(2)}) copy-start(f32[16,128]{1,0:T(8,128)S(1)} %get-tuple-element.409) | copy-start | bytes 24580
  59.0 20.8 %copy-start.68 = (f32[16,128]{1,0:T(8,128)}, f32[16,128]{1,0:T(8,128)S(1)}, u32[]{:S(2)}) copy-start(f32[16,128]{1,0:T(8,128)S(1)} %get-tuple-element.617) | copy-start | bytes 24580
  59.0 22.2 %copy-start.67 = (f32[16,128]{1,0:T(8,128)}, f32[16,128]{1,0:T(8,128)S(1)}, u32[]{:S(2)}) copy-start(f32[16,128]{1,0:T(8,128)S(1)} %get-tuple-element.411) | copy-start | bytes 24580
  59.1 22.2 %copy-start.32 = (f32[16,128]{1,0:T(8,128)}, f32[16,128]{1,0:T(8,128)S(1)}, u32[]{:S(2)}) copy-start(f32[16,128]{1,0:T(8,128)S(1)} %get-tuple-element.413) | copy-start | bytes 24580
  59.7 20.1 %copy-start.42 = (f32[1,16,128]{2,1,0:T(8,128)}, f32[1,16,128]{2,1,0:T(8,128)S(1)}, u32[]{:S(2)}) copy-start(f32[1,16,128]{2,1,0:T(8,128)S(1)} %get-tuple-element.418) | copy-start | bytes 24580
  59.7 21.6 %copy-start.30 = (f32[16,128]{1,0:T(8,128)}, f32[16,128]{1,0:T(8,128)S(1)}, u32[]{:S(2)}) copy-start(f32[16,128]{1,0:T(8,128)S(1)} %get-tuple-element.417) | copy-start | bytes 24580
  60.4 20.9 %copy-start.28 = (f32[16,128]{1,0:T(8,128)}, f32[16,128]{1,0:T(8,128)S(1)}, u32[]{:S(2)}) copy-start(f32[16,128]{1,0:T(8,128)S(1)} %get-tuple-element.421) | copy-start | bytes 24580
  61.0 18.9 %copy-start.43 = (f32[1,16,128]{2,1,0:T(8,128)}, f32[1,16,128]{2,1,0:T(8,128)S(1)}, u32[]{:S(2)}) copy-start(f32[1,16,128]{2,1,0:T(8,128)S(1)} %get-tuple-element.426) | copy-start | bytes 24580
  61.0 20.3 %copy-start.26 = (f32[16,128]{1,0:T(8,128)}, f32[16,128]{1,0:T(8,128)S(1)}, u32[]{:S(2)}) copy-start(f32[16,128]{1,0:T(8,128)S(1)} %get-tuple-element.425) | copy-start | bytes 24580
  61.6 19.7 %copy-start.24 = (f32[16,128]{1,0:T(8,128)}, f32[16,128]{1,0:T(8,128)S(1)}, u32[]{:S(2)}) copy-start(f32[16,128]{1,0:T(8,128)S(1)} %get-tuple-element.429) | copy-start | bytes 24580
  62.3 17.6 %copy-start.44 = (f32[1,16,128]{2,1,0:T(8,128)}, f32[1,16,128]{2,1,0:T(8,128)S(1)}, u32[]{:S(2)}) copy-start(f32[1,16,128]{2,1,0:T(8,128)S(1)} %get-tuple-element.434) | copy-start | bytes 24580
  62.3 19.0 %copy-start.22 = (f32[16,128]{1,0:T(8,128)}, f32[16,128]{1,0:T(8,128)S(1)}, u32[]{:S(2)}) copy-start(f32[16,128]{1,0:T(8,128)S(1)} %get-tuple-element.433) | copy-start | bytes 24580
  62.9 18.4 %copy-start.20 = (f32[16,128]{1,0:T(8,128)}, f32[16,128]{1,0:T(8,128)S(1)}, u32[]{:S(2)}) copy-start(f32[16,128]{1,0:T(8,128)S(1)} %get-tuple-element.437) | copy-start | bytes 24580
  63.6 16.3 %copy-start.45 = (f32[1,16,128]{2,1,0:T(8,128)}, f32[1,16,128]{2,1,0:T(8,128)S(1)}, u32[]{:S(2)}) copy-start(f32[1,16,128]{2,1,0:T(8,128)S(1)} %get-tuple-element.442) | copy-start | bytes 24580
  63.6 17.8 %copy-start.18 = (f32[16,128]{1,0:T(8,128)}, f32[16,128]{1,0:T(8,128)S(1)}, u32[]{:S(2)}) copy-start(f32[16,128]{1,0:T(8,128)S(1)} %get-tuple-element.441) | copy-start | bytes 24580
  64.2 17.1 %copy-start.16 = (f32[16,128]{1,0:T(8,128)}, f32[16,128]{1,0:T(8,128)S(1)}, u32[]{:S(2)}) copy-start(f32[16,128]{1,0:T(8,128)S(1)} %get-tuple-element.445) | copy-start | bytes 24580
  64.8 15.1 %copy-start.46 = (f32[1,16,128]{2,1,0:T(8,128)}, f32[1,16,128]{2,1,0:T(8,128)S(1)}, u32[]{:S(2)}) copy-start(f32[1,16,128]{2,1,0:T(8,128)S(1)} %get-tuple-element.450) | copy-start | bytes 24580
  64.8 16.5 %copy-start.14 = (f32[16,128]{1,0:T(8,128)}, f32[16,128]{1,0:T(8,128)S(1)}, u32[]{:S(2)}) copy-start(f32[16,128]{1,0:T(8,128)S(1)} %get-tuple-element.449) | copy-start | bytes 24580
  65.5 15.9 %copy-start.10 = (f32[16,128]{1,0:T(8,128)}, f32[16,128]{1,0:T(8,128)S(1)}, u32[]{:S(2)}) copy-start(f32[16,128]{1,0:T(8,128)S(1)} %get-tuple-element.453) | copy-start | bytes 24580
  66.1 13.8 %copy-start.47 = (f32[1,16,128]{2,1,0:T(8,128)}, f32[1,16,128]{2,1,0:T(8,128)S(1)}, u32[]{:S(2)}) copy-start(f32[1,16,128]{2,1,0:T(8,128)S(1)} %get-tuple-element.458) | copy-start | bytes 24580
  66.1 15.2 %copy-start.8 = (f32[16,128]{1,0:T(8,128)}, f32[16,128]{1,0:T(8,128)S(1)}, u32[]{:S(2)}) copy-start(f32[16,128]{1,0:T(8,128)S(1)} %get-tuple-element.457) | copy-start | bytes 24580
  66.8 14.6 %copy-start.6 = (f32[16,128]{1,0:T(8,128)}, f32[16,128]{1,0:T(8,128)S(1)}, u32[]{:S(2)}) copy-start(f32[16,128]{1,0:T(8,128)S(1)} %get-tuple-element.461) | copy-start | bytes 24580
  67.4 12.5 %copy-start.48 = (f32[1,16,128]{2,1,0:T(8,128)}, f32[1,16,128]{2,1,0:T(8,128)S(1)}, u32[]{:S(2)}) copy-start(f32[1,16,128]{2,1,0:T(8,128)S(1)} %get-tuple-element.466) | copy-start | bytes 24580
  67.4 14.0 %copy-start.4 = (f32[16,128]{1,0:T(8,128)}, f32[16,128]{1,0:T(8,128)S(1)}, u32[]{:S(2)}) copy-start(f32[16,128]{1,0:T(8,128)S(1)} %get-tuple-element.465) | copy-start | bytes 24580
  98.3 12.5 %copy-start.21 = (f32[16,128]{1,0:T(8,128)S(1)}, f32[16,128]{1,0:T(8,128)}, u32[]{:S(2)}) copy-start(f32[16,128]{1,0:T(8,128)} %copy-done.20) | copy-start | bytes 24580
  98.3 13.7 %copy-start.19 = (f32[16,128]{1,0:T(8,128)S(1)}, f32[16,128]{1,0:T(8,128)}, u32[]{:S(2)}) copy-start(f32[16,128]{1,0:T(8,128)} %copy-done.18) | copy-start | bytes 24580
  98.3 14.9 %copy-start.17 = (f32[16,128]{1,0:T(8,128)S(1)}, f32[16,128]{1,0:T(8,128)}, u32[]{:S(2)}) copy-start(f32[16,128]{1,0:T(8,128)} %copy-done.16) | copy-start | bytes 24580
  98.3 16.1 %copy-start.15 = (f32[16,128]{1,0:T(8,128)S(1)}, f32[16,128]{1,0:T(8,128)}, u32[]{:S(2)}) copy-start(f32[16,128]{1,0:T(8,128)} %copy-done.14) | copy-start | bytes 24580
  98.3 17.3 %copy-start.11 = (f32[16,128]{1,0:T(8,128)S(1)}, f32[16,128]{1,0:T(8,128)}, u32[]{:S(2)}) copy-start(f32[16,128]{1,0:T(8,128)} %copy-done.10) | copy-start | bytes 24580
  101.5 15.3 %copy-start.9 = (f32[16,128]{1,0:T(8,128)S(1)}, f32[16,128]{1,0:T(8,128)}, u32[]{:S(2)}) copy-start(f32[16,128]{1,0:T(8,128)} %copy-done.8) | copy-start | bytes 24580
  101.5 16.5 %copy-start.7 = (f32[16,128]{1,0:T(8,128)S(1)}, f32[16,128]{1,0:T(8,128)}, u32[]{:S(2)}) copy-start(f32[16,128]{1,0:T(8,128)} %copy-done.6) | copy-start | bytes 24580
  101.6 17.7 %copy-start.5 = (f32[16,128]{1,0:T(8,128)S(1)}, f32[16,128]{1,0:T(8,128)}, u32[]{:S(2)}) copy-start(f32[16,128]{1,0:T(8,128)} %copy-done.4) | copy-start | bytes 24580
  101.6 23.8 %copy-start.53 = (f32[16,128]{1,0:T(8,128)S(1)}, f32[16,128]{1,0:T(8,128)}, u32[]{:S(2)}) copy-start(f32[16,128]{1,0:T(8,128)} %copy-done.52) | copy-start | bytes 24580
  101.6 25.0 %copy-start.54 = (f32[3,16,128]{2,1,0:T(8,128)S(1)}, f32[3,16,128]{2,1,0:T(8,128)}, u32[]{:S(2)}) copy-start(f32[3,16,128]{2,1,0:T(8,128)} %get-tuple-element.384) | copy-start | bytes 73732
  101.6 25.6 %copy-start.64 = (f32[3,16,128]{2,1,0:T(8,128)S(1)}, f32[3,16,128]{2,1,0:T(8,128)}, u32[]{:S(2)}) copy-start(f32[3,16,128]{2,1,0:T(8,128)} %get-tuple-element.404) | copy-start | bytes 73732
  101.6 26.8 %copy-start.63 = (f32[3,16,128]{2,1,0:T(8,128)S(1)}, f32[3,16,128]{2,1,0:T(8,128)}, u32[]{:S(2)}) copy-start(f32[3,16,128]{2,1,0:T(8,128)} %get-tuple-element.403) | copy-start | bytes 73732
  101.6 28.0 %copy-start.62 = (f32[3,16,128]{2,1,0:T(8,128)S(1)}, f32[3,16,128]{2,1,0:T(8,128)}, u32[]{:S(2)}) copy-start(f32[3,16,128]{2,1,0:T(8,128)} %get-tuple-element.402) | copy-start | bytes 73732
  102.2 28.6 %copy-start.61 = (f32[3,16,128]{2,1,0:T(8,128)S(1)}, f32[3,16,128]{2,1,0:T(8,128)}, u32[]{:S(2)}) copy-start(f32[3,16,128]{2,1,0:T(8,128)} %get-tuple-element.401) | copy-start | bytes 73732
  103.4 28.6 %copy-start.60 = (f32[3,16,128]{2,1,0:T(8,128)S(1)}, f32[3,16,128]{2,1,0:T(8,128)}, u32[]{:S(2)}) copy-start(f32[3,16,128]{2,1,0:T(8,128)} %get-tuple-element.400) | copy-start | bytes 73732
  104.7 28.6 %copy-start.59 = (f32[3,16,128]{2,1,0:T(8,128)S(1)}, f32[3,16,128]{2,1,0:T(8,128)}, u32[]{:S(2)}) copy-start(f32[3,16,128]{2,1,0:T(8,128)} %get-tuple-element.399) | copy-start | bytes 73732
  105.9 28.6 %copy-start.58 = (f32[3,16,128]{2,1,0:T(8,128)S(1)}, f32[3,16,128]{2,1,0:T(8,128)}, u32[]{:S(2)}) copy-start(f32[3,16,128]{2,1,0:T(8,128)} %get-tuple-element.398) | copy-start | bytes 73732
  107.1 28.6 %copy-start.57 = (f32[3,16,128]{2,1,0:T(8,128)S(1)}, f32[3,16,128]{2,1,0:T(8,128)}, u32[]{:S(2)}) copy-start(f32[3,16,128]{2,1,0:T(8,128)} %get-tuple-element.397) | copy-start | bytes 73732
  108.3 28.6 %copy-start.56 = (f32[3,16,128]{2,1,0:T(8,128)S(1)}, f32[3,16,128]{2,1,0:T(8,128)}, u32[]{:S(2)}) copy-start(f32[3,16,128]{2,1,0:T(8,128)} %get-tuple-element.396) | copy-start | bytes 73732
  109.5 28.6 %copy-start.55 = (f32[3,16,128]{2,1,0:T(8,128)S(1)}, f32[3,16,128]{2,1,0:T(8,128)}, u32[]{:S(2)}) copy-start(f32[3,16,128]{2,1,0:T(8,128)} %get-tuple-element.395) | copy-start | bytes 73732
  (12 other events, 87.2 us)
where the time goes:
time: 144 us; the launch traced here: 142 us
  other arithmetic  73.2 us (51%)
  local copies, waits for them, and re-layouts  25 us (17%)
  starting transfers between devices  18.1 us (13%)
  blocking collectives  13.5 us (9%)
  waiting for transfers between devices  9.69 us (7%)
  between operations  1.73 us (1%)
    unnamed x39, other arithmetic  23.9 us
    unnamed x173, local copies, waits for them, and re-layouts  20 us
    mul x43, other arithmetic, backward(): value = dd - cc[None] * after  15 us
    all_gather x1, blocking collectives, shards(): every = lax.all_gather(packed, 'line', axis=0, tiled=True)  13.5 us
    ppermute x3, starting transfers between devices, with_halo(): lax.ppermute(tail, axis, [(i, (i + 1) % count) for i in range(ends)])  9.91 us
    ppermute x3, starting transfers between devices, with_halo(): lax.ppermute(head, axis, [((i + 1) % count, i) for i in range(ends)])  8.14 us
    ppermute x3, waiting for transfers between devices, with_halo(): lax.ppermute(head, axis, [((i + 1) % count, i) for i in range(ends)])  7.89 us
    convert_element_type x1, other arithmetic, shards(): residual.astype(jnp.bfloat16)  7.81 us
  transfers between devices with their start and end apart: 6, of which 4 were waited for; matrix products, arithmetic and copies ran while one was open for 1% of the time, Pallas kernels for 0%

commit v1 on v0

v1 whole, which is shorter than its diff:
```python
import functools

import jax
import jax.numpy as jnp
from jax import lax
from jax.experimental import pallas as pl
from jax.experimental.pallas import tpu as pltpu
from jax.sharding import PartitionSpec as P

MESH = pl.DeviceIdType.MESH
RUNS = 8
STEPS = 8
F32 = jnp.float32


def recip(x):
    y = pltpu.reciprocal(x, approx=True)
    return y * (2.0 - x * y)


def conductance(first, second):
    return 2.0 * first * second * recip(first + second)


def eliminate(left, ground, right):
    inv = recip(left + ground + right)
    return left * inv, right * inv, inv


def spot(run, step):
    return pl.ds((run * STEPS + step) * 16, 16)


def read(ref, step):
    return jnp.stack([ref[spot(run, step), :] for run in range(RUNS)])


def write(ref, step, value):
    for run in range(RUNS):
        ref[spot(run, step), :] = value[run]


def kernel(
    count_line, count_chip, count_layer,
    temp_hbm, power_hbm, weight_hbm, lut, label_hbm,
    res_hbm, heat_hbm,
    temp, power, weight, label, cond, res, heat,
    gx, coef_t, coef_u, coef_q,
    line_send, line_recv, layer_send, layer_recv, chip_send, chip_recv,
    mats, rights,
    in_sem, out_sem, halo_send_sem, halo_recv_sem,
    mat_send_sem, mat_recv_sem, rhs_send_sem, rhs_recv_sem,
):
    line = lax.axis_index("line")
    chip = lax.axis_index("chip")
    layer = lax.axis_index("layer")
    depth, width = 16, 128

    loads = [
        pltpu.make_async_copy(src, dst, in_sem.at[n])
        for n, (src, dst) in enumerate(
            ((label_hbm, label), (temp_hbm, temp), (power_hbm, power), (weight_hbm, weight))
        )
    ]
    for load in loads:
        load.start()

    line_recv[...] = jnp.zeros_like(line_recv)
    layer_recv[...] = jnp.zeros_like(layer_recv)
    chip_recv[...] = jnp.zeros_like(chip_recv)

    has = (
        line > 0, line < count_line - 1,
        layer > 0, layer < count_layer - 1,
        chip > 0, chip < count_chip - 1,
    )
    where = (
        {"line": line - 1}, {"line": line + 1},
        {"layer": layer - 1}, {"layer": layer + 1},
        {"chip": chip - 1}, {"chip": chip + 1},
    )
    sends = (line_send, line_send, layer_send, layer_send, chip_send, chip_send)
    recvs = (line_recv, line_recv, layer_recv, layer_recv, chip_recv, chip_recv)

    barrier = pltpu.get_barrier_semaphore()
    peers = [lax.rem(line + r, count_line) for r in range(1, count_line)]
    for peer in peers:
        pl.semaphore_signal(barrier, inc=1, device_id={"line": peer}, device_id_type=MESH)
    for side in range(2, 6):
        @pl.when(has[side])
        def _():
            pl.semaphore_signal(barrier, inc=1, device_id=where[side], device_id_type=MESH)

    def halo(side):
        return pltpu.make_async_remote_copy(
            src_ref=sends[side] if side >= 4 else sends[side].at[side % 2],
            dst_ref=recvs[side].at[1 - side % 2],
            send_sem=halo_send_sem.at[side],
            recv_sem=halo_recv_sem.at[side - side % 2 + 1 - side % 2],
            device_id=where[side],
            device_id_type=MESH,
        )

    def halo_start(side):
        @pl.when(has[side])
        def _():
            halo(side).start()

    def halo_landed(side):
        @pl.when(has[side])
        def _():
            pltpu.make_async_remote_copy(
                src_ref=sends[side] if side >= 4 else sends[side].at[side % 2],
                dst_ref=recvs[side].at[side % 2],
                send_sem=halo_send_sem.at[side],
                recv_sem=halo_recv_sem.at[side],
                device_id=where[side],
                device_id_type=MESH,
            ).wait_recv()

    values = [lut[n] for n in range(8)]
    loads[0].wait()

    def look_up(tags):
        odd = (tags & 1) == 1
        two = (tags & 2) == 2
        four = tags >= 4
        pairs = [jnp.where(odd, values[2 * n + 1], values[2 * n]) for n in range(4)]
        halves = [jnp.where(two, pairs[2 * n + 1], pairs[2 * n]) for n in range(2)]
        return jnp.where(four, halves[1], halves[0])

    for i in range(STEPS):
        write(cond, i, look_up(label[:, i]))
    loads[1].wait()
    start, stop = spot(0, 0), spot(RUNS - 1, STEPS - 1)
    line_send[0, 0] = temp[start, :]
    line_send[0, 1] = cond[start, :]
    line_send[1, 0] = temp[stop, :]
    line_send[1, 1] = cond[stop, :]
    rows = RUNS * STEPS
    for end, first in ((0, 0), (1, depth - 1)):
        layer_send[end, 0] = temp[pl.ds(first, rows, stride=depth), :]
        layer_send[end, 1] = cond[pl.ds(first, rows, stride=depth), :]

    total = count_line - 1 + sum(side.astype(jnp.int32) for side in has[2:])
    pl.semaphore_wait(barrier, total)
    for side in range(4):
        halo_start(side)

    lane = lax.broadcasted_iota(jnp.int32, (1, 1, width), 2)
    packed = jnp.zeros((RUNS, depth, width), F32)
    for i in range(STEPS):
        packed = jnp.where(
            lane // 2 == 2 * i, pltpu.roll(read(temp, i), 4 * i + 1, 2),
            jnp.where(lane // 2 == 2 * i + 1, pltpu.roll(read(cond, i), 4 * i + 3, 2), packed),
        )
    packed = packed.reshape(2, 4, depth, width)
    dense = packed[:, 0]
    for k in range(1, 4):
        dense = jnp.where(lane // 32 == k, pltpu.roll(packed[:, k], 32 * k, 2), dense)
    chip_send[...] = dense
    halo_start(4)
    halo_start(5)

    loads[2].wait()
    row = lax.broadcasted_iota(jnp.int32, (1, depth, 1), 1)
    for i in range(STEPS):
        heat_here, k_here = read(temp, i), read(cond, i)
        flow_y = jnp.where(
            lane == width - 1, 0.0,
            conductance(k_here, pltpu.roll(k_here, width - 1, 2))
            * (heat_here - pltpu.roll(heat_here, width - 1, 2)),
        )
        flow_z = jnp.where(
            row == depth - 1, 0.0,
            conductance(k_here, pltpu.roll(k_here, depth - 1, 1))
            * (heat_here - pltpu.roll(heat_here, depth - 1, 1)),
        )
        write(res, i, (
            power[:, i]
            - (flow_y - pltpu.roll(flow_y, 1, 2))
            - (flow_z - pltpu.roll(flow_z, 1, 1))
        ))

    halo_landed(0)
    halo_landed(1)
    first_t, first_k = temp[start, :], cond[start, :]
    last_t, last_k = temp[stop, :], cond[stop, :]
    g_left = conductance(first_k, line_recv[0, 1])
    g_right = conductance(last_k, line_recv[1, 1])
    flow_left = g_left * (line_recv[0, 0] - first_t)
    flow_right = g_right * (last_t - line_recv[1, 0])
    flow = None
    for i in range(STEPS):
        heat_here, k_here = read(temp, i), read(cond, i)
        if i < STEPS - 1:
            g = conductance(k_here, read(cond, i + 1))
            flow_on = g * (heat_here - read(temp, i + 1))
        else:
            next_k = jnp.concatenate([read(cond, 0)[1:], line_recv[1:2, 1]], axis=0)
            next_t = jnp.concatenate([read(temp, 0)[1:], line_recv[1:2, 0]], axis=0)
            g = conductance(k_here, next_k)
            flow_on = g * (heat_here - next_t)
        gx[:, i] = g
        if i == 0:
            write(res, i, read(res, i) - flow_on)
        else:
            write(res, i, read(res, i) + flow - flow_on)
        flow = flow_on
    write(res, 0, read(res, 0) + jnp.concatenate([flow_left[None], flow[:-1]], axis=0))

    loads[3].wait()
    ya, c, yb = weight[:, 0], gx[:, 0], weight[:, 1]
    for i in range(1, STEPS - 1):
        u, t, inv = eliminate(c, yb, gx[:, i])
        ya = ya + u * yb
        c = c * t
        yb = weight[:, i + 1] + t * yb
        coef_u[:, i] = u
        coef_t[:, i] = t
        coef_q[:, i] = inv
    join = gx[:, STEPS - 1]
    tree = []
    while ya.shape[0] > 1:
        half = ya.shape[0] // 2
        ya_l, ya_r = (ya.reshape(half, 2, depth, width)[:, n] for n in range(2))
        yb_l, yb_r = (yb.reshape(half, 2, depth, width)[:, n] for n in range(2))
        c_l, c_r = (c.reshape(half, 2, depth, width)[:, n] for n in range(2))
        g, join = (join.reshape(half, 2, depth, width)[:, n] for n in range(2))
        first = eliminate(c_l, yb_l, g)
        u, t, _ = first
        ya = ya_l + u * yb_l
        c = c_l * t
        mid = ya_r + t * yb_l
        second = eliminate(c, mid, c_r)
        u, t, _ = second
        ya = ya + u * mid
        c = c * t
        yb = yb_r + t * mid
        tree.append((first, second))
    mats[line, 0] = ya[0]
    mats[line, 1] = c[0]
    mats[line, 2] = yb[0]
    mats[line, 3] = g_left

    def spread(block, send_sem, recv_sem):
        return [
            pltpu.make_async_remote_copy(
                src_ref=block.at[line],
                dst_ref=block.at[line],
                send_sem=send_sem.at[r],
                recv_sem=recv_sem.at[r],
                device_id={"line": peer},
                device_id_type=MESH,
            )
            for r, peer in enumerate(peers)
        ]

    def landed(block, send_sem, recv_sem):
        for r in range(count_line - 1):
            source = lax.rem(line + count_line - 1 - r, count_line)
            pltpu.make_async_remote_copy(
                src_ref=block.at[source],
                dst_ref=block.at[source],
                send_sem=send_sem.at[r],
                recv_sem=recv_sem.at[r],
                device_id={"line": source},
                device_id_type=MESH,
            ).wait_recv()

    mat_copies = spread(mats, mat_send_sem, mat_recv_sem)
    for copy in mat_copies:
        copy.start()

    halo_landed(2)
    halo_landed(3)
    is_top = layer == count_layer - 1
    for end, first in ((0, 0), (1, depth - 1)):
        own_t, own_k = layer_send[end, 0], layer_send[end, 1]
        g = conductance(own_k, layer_recv[end, 1])
        if end == 1:
            g = jnp.where(is_top, own_k, g)
        face = pl.ds(first, rows, stride=depth)
        res[face, :] = res[face, :] - g * (own_t - layer_recv[end, 0])

    halo_landed(4)
    halo_landed(5)
    own = chip_send[...]
    other = jnp.where(
        lane % 2 == 0, pltpu.roll(chip_recv[1], width - 1, 2), pltpu.roll(chip_recv[0], 1, 2)
    )
    edge = jnp.where(
        lane % 4 < 2,
        conductance(pltpu.roll(own, width - 2, 2), pltpu.roll(other, width - 2, 2))
        * (own - other),
        0.0,
    )
    edges = jnp.stack(
        [edge] + [pltpu.roll(edge, width - 32 * k, 2) for k in range(1, 4)], axis=1
    ).reshape(RUNS, depth, width)
    at_edge = (lane == 0) | (lane == width - 1)
    rounded = []
    for i in range(STEPS):
        total_res = read(res, i) - jnp.where(
            at_edge, pltpu.roll(edges, width - 1 - 4 * i, 2), 0.0
        )
        write(res, i, total_res)
        right = total_res.astype(jnp.bfloat16).astype(F32)
        if i == 0:
            ra = right
        elif i == 1:
            rb = right
        else:
            ra = ra + coef_u[:, i - 1] * rb
            held = coef_t[:, i - 1] * rb
            coef_q[:, i - 1] = coef_q[:, i - 1] * rb
            rb = right + held
    res_copy = pltpu.make_async_copy(res, res_hbm, out_sem.at[0])
    res_copy.start()

    held = []
    for (u1, t1, inv1), (u2, t2, inv2) in tree:
        half = ra.shape[0] // 2
        ra_l, ra_r = (ra.reshape(half, 2, depth, width)[:, n] for n in range(2))
        rb_l, rb_r = (rb.reshape(half, 2, depth, width)[:, n] for n in range(2))
        mid = ra_r + t1 * rb_l
        held.append((inv1 * rb_l, inv2 * mid))
        ra = ra_l + u1 * rb_l + u2 * mid
        rb = rb_r + t2 * mid
    rights[line, 0] = ra[0]
    rights[line, 1] = rb[0]
    rhs_copies = spread(rights, rhs_send_sem, rhs_recv_sem)
    for copy in rhs_copies:
        copy.start()

    landed(mats, mat_send_sem, mat_recv_sem)
    zero = jnp.zeros((depth, width), F32)
    before, after = zero, zero
    up, down = [], []
    for j in range(count_line - 1):
        a, b, cc = mats[j, 0], mats[j, 2], mats[j, 1]
        if j > 0:
            g = mats[j, 3]
            v = g * recip(g + before)
            a = a + v * before
        else:
            v = zero
        u = cc * recip(a + cc)
        before = jnp.where(j < line, b + u * a, before)
        up.append((u, v))
        n = count_line - 1 - j
        a, b, cc = mats[n, 0], mats[n, 2], mats[n, 1]
        if j > 0:
            g = mats[n + 1, 3]
            v = g * recip(g + after)
            b = b + v * after
        else:
            v = zero
        u = cc * recip(b + cc)
        after = jnp.where(n > line, a + u * b, after)
        down.append((u, v))
    ya, c, yb = ya[0], c[0], yb[0]
    v_left = jnp.where(line > 0, g_left * recip(g_left + before + 1e-30), 0.0)
    v_right = jnp.where(
        line < count_line - 1, g_right * recip(g_right + after + 1e-30), 0.0
    )
    a = ya + v_left * before
    b = yb + v_right * after
    inv = recip(a * b + c * (a + b))
    from_a, from_b, cross = (b + c) * inv, (a + c) * inv, c * inv

    landed(rights, rhs_send_sem, rhs_recv_sem)
    left_in, right_in = zero, zero
    for j in range(count_line - 1):
        u, v = up[j]
        new = rights[j, 1] + u * (rights[j, 0] + v * left_in)
        left_in = jnp.where(j < line, new, left_in)
        n = count_line - 1 - j
        u, v = down[j]
        new = rights[n, 0] + u * (rights[n, 1] + v * right_in)
        right_in = jnp.where(n > line, new, right_in)
    ra = ra[0] + v_left * left_in
    rb = rb[0] + v_right * right_in
    xa = (from_a * ra + cross * rb)[None]
    xb = (cross * ra + from_b * rb)[None]

    for ((u1, t1, _), (u2, t2, _)), (q1, q2) in zip(reversed(tree), reversed(held)):
        xr = q2 + u2 * xa + t2 * xb
        xl = q1 + u1 * xa + t1 * xr
        size = 2 * xa.shape[0]
        xa = jnp.stack([xa, xr], axis=1).reshape(size, depth, width)
        xb = jnp.stack([xl, xb], axis=1).reshape(size, depth, width)
    heat[:, 0] = weight[:, 0] * xa
    heat[:, STEPS - 1] = weight[:, STEPS - 1] * xb
    x = xb
    for i in range(STEPS - 2, 0, -1):
        x = coef_q[:, i] + coef_u[:, i] * xa + coef_t[:, i] * x
        heat[:, i] = weight[:, i] * x
    heat_copy = pltpu.make_async_copy(heat, heat_hbm, out_sem.at[1])
    heat_copy.start()

    for side in range(6):
        @pl.when(has[side])
        def _():
            halo(side).wait_send()
    for copy in mat_copies + rhs_copies:
        copy.wait_send()
    res_copy.wait()
    heat_copy.wait()


def shards(counts, warmth_field, power_input, inertia_weight, conductivity_lookup, substance_label):
    depth, width = warmth_field.shape[1:]
    shape = (RUNS, STEPS, depth, width)
    vmem = pltpu.VMEM
    whole = vmem(shape, F32)
    others = counts[0] - 1
    dma = pltpu.SemaphoreType.DMA
    any_space = pl.BlockSpec(memory_space=pl.ANY)
    flat = (RUNS * STEPS * depth, width)
    rows = vmem(flat, F32)
    residual, heat_rate = pl.pallas_call(
        functools.partial(kernel, *counts),
        out_shape=(jax.ShapeDtypeStruct(flat, F32), jax.ShapeDtypeStruct(shape, F32)),
        in_specs=[any_space, any_space, any_space, pl.BlockSpec(memory_space=pltpu.SMEM), any_space],
        out_specs=(any_space, any_space),
        scratch_shapes=[
            rows, whole, whole, vmem(shape, jnp.int32), rows, rows, whole,
            whole, whole, whole, whole,
            vmem((2, 2, depth, width), F32), vmem((2, 2, depth, width), F32),
            vmem((2, 2, RUNS * STEPS, width), F32), vmem((2, 2, RUNS * STEPS, width), F32),
            vmem((2, depth, width), F32), vmem((2, 2, depth, width), F32),
            vmem((counts[0], 4, depth, width), F32), vmem((counts[0], 2, depth, width), F32),
            dma((4,)), dma((2,)), dma((6,)), dma((6,)),
            dma((others,)), dma((others,)), dma((others,)), dma((others,)),
        ],
        compiler_params=pltpu.CompilerParams(
            collective_id=0, has_side_effects=True, vmem_limit_bytes=32 * 1024 * 1024
        ),
    )(
        warmth_field.reshape(flat), power_input.reshape(shape), inertia_weight.reshape(shape),
        conductivity_lookup, substance_label.reshape(shape),
    )
    return residual.reshape(warmth_field.shape), heat_rate.reshape(warmth_field.shape)


def solution(mesh):
    counts = tuple(mesh.shape[axis] for axis in ("line", "chip", "layer"))
    spec = P("line", "layer", "chip")
    return jax.shard_map(
        functools.partial(shards, counts),
        mesh=mesh,
        in_specs=(spec, spec, spec, P(), spec),
        out_specs=(spec, spec),
        check_vma=False,
    )
```

time: 144 us -> 27.3 us (0.19); the launches traced: 142 us -> 27 us
  other arithmetic: 73.2 us -> 0 us
  Pallas kernels: 0 us -> 19.9 us
  local copies, waits for them, and re-layouts: 25 us -> 6.4 us
  starting transfers between devices: 18.1 us -> 0 us
  blocking collectives: 13.5 us -> 0 us
  waiting for transfers between devices: 9.69 us -> 0 us
    unnamed x39 -> x0, other arithmetic: 23.9 us -> none
    pallas_call x0 -> x1, Pallas kernels: none -> 19.9 us  [shards(): pl.pallas_call(functools.partial(kernel, *counts), out_shape=(jax.ShapeDt...]
    ppermute x6 -> x0, starting transfers between devices: 18.1 us -> none  [the longest x3 9.91 us: with_halo(): lax.ppermute(tail, axis, [(i, (i + 1) % count) for i in range(ends)])]
    mul x44 -> x0, other arithmetic: 17.4 us -> none  [the longest x43 15 us: backward(): value = dd - cc[None] * after]
    unnamed x173 -> x12, local copies, waits for them, and re-layouts: 20 us -> 6.4 us
    all_gather x1 -> x0, blocking collectives: 13.5 us -> none  [shards(): every = lax.all_gather(packed, 'line', axis=0, tiled=True)]
    ppermute x6 -> x0, waiting for transfers between devices: 9.69 us -> none  [the longest x3 7.89 us: with_halo(): lax.ppermute(head, axis, [((i + 1) % count, i) for i in range(ends)])]
    convert_element_type x1 -> x0, other arithmetic: 7.81 us -> none  [shards(): residual.astype(jnp.bfloat16)]
  transfers between devices with their start and end apart: 6 -> 0, of which waited for: 4 -> 0; matrix products, arithmetic and copies ran while one was open for 1% -> 0% of each run, Pallas kernels for 0% -> 0%
where the time goes in v1:
time: 27.3 us; the launch traced here: 27 us
  Pallas kernels  19.9 us (73%)
  local copies, waits for them, and re-layouts  6.4 us (23%)
  between operations  0.65 us (2%)
    pallas_call x1, Pallas kernels, shards(): pl.pallas_call(functools.partial(kernel, *counts), out_shape=(jax.ShapeDt...  19.9 us
    unnamed x12, local copies, waits for them, and re-layouts  6.4 us

profile of v1, /device:TPU:1, one launch (start us, length us, event | category | flops | bytes accessed | tf_op | source)
XLA Modules:
  0.0 27.0 jit_solution(7851606901047508253)
XLA Ops:
  0.6 0.0 copy-start.4
  0.6 0.6 %copy-done.4 = f32[8]{0:T(128)S(1)} copy-done((f32[8]{0:T(128)S(1)}, f32[8]{0:T(128)}, u32[]{:S(2)}) %copy-start.4) | copy-done | bytes 56
  1.3 0.0 copy-start
  1.3 1.0 %copy-done = f32[64,16,128]{2,1,0:T(8,128)S(1)} copy-done((f32[64,16,128]{2,1,0:T(8,128)S(1)}, f32[64,16,128]{2,1,0:T(8,128)}, u32[]{:S(2)}) %copy-start) | copy-done | bytes 524312
  2.3 0.0 copy-start.1
  2.3 1.0 %copy-done.1 = f32[64,16,128]{2,1,0:T(8,128)S(1)} copy-done((f32[64,16,128]{2,1,0:T(8,128)S(1)}, f32[64,16,128]{2,1,0:T(8,128)}, u32[]{:S(2)}) %copy-start.1) | copy-done | bytes 524312
  3.4 0.0 copy-start.2
  3.4 1.0 %copy-done.2 = f32[64,16,128]{2,1,0:T(8,128)S(1)} copy-done((f32[64,16,128]{2,1,0:T(8,128)S(1)}, f32[64,16,128]{2,1,0:T(8,128)}, u32[]{:S(2)}) %copy-start.2) | copy-done | bytes 524312
  4.4 0.0 copy-start.3
  4.4 1.0 %copy-done.3 = s32[64,16,128]{2,1,0:T(8,128)S(1)} copy-done((s32[64,16,128]{2,1,0:T(8,128)S(1)}, s32[64,16,128]{2,1,0:T(8,128)}, u32[]{:S(2)}) %copy-start.3) | copy-done | bytes 524312
  5.5 19.9 %shard_map.68 = (f32[1024,128]{1,0:T(8,128)S(1)}, f32[8,8,16,128]{3,2,1,0:T(8,128)S(1)}) custom-call(f32[1024,128]{1,0:T(8,128)S(1)} %bitcast.6, f32[8,8,16,128]{3,2,1,0:T(8,128)S(1)} %bitcast.7, f32[8,8,16,128]{3,2,1,0:T(8,128)S(1)} %bitcast.8, f32[8]{0:T(128)S(1)} %copy-done.4, s32[8,8,16,128]{3,2,1,0:T(8,128)S(1)} %bitcast.9), custom_call_target="tpu_custom_call" | custom-call | tf_op jit(solution)/shard_map/pallas_call | solution.py:422
  25.4 0.8 %copy.9 = f32[64,16,128]{2,1,0:T(8,128)} copy(f32[64,16,128]{2,1,0:T(8,128)S(1)} %bitcast.11) | data formatting | bytes 1048576
  26.2 0.8 %copy.10 = f32[64,16,128]{2,1,0:T(8,128)} copy(f32[64,16,128]{2,1,0:T(8,128)S(1)} %bitcast.10) | data formatting | bytes 1048576
Async XLA Ops:
  0.6 0.7 %copy-start.4 = (f32[8]{0:T(128)S(1)}, f32[8]{0:T(128)}, u32[]{:S(2)}) copy-start(f32[8]{0:T(128)} %lut.1) | copy-start | bytes 100
  1.3 1.0 %copy-start = (f32[64,16,128]{2,1,0:T(8,128)S(1)}, f32[64,16,128]{2,1,0:T(8,128)}, u32[]{:S(2)}) copy-start(f32[64,16,128]{2,1,0:T(8,128)} %param.5) | copy-start | bytes 1572868
  2.3 1.0 %copy-start.1 = (f32[64,16,128]{2,1,0:T(8,128)S(1)}, f32[64,16,128]{2,1,0:T(8,128)}, u32[]{:S(2)}) copy-start(f32[64,16,128]{2,1,0:T(8,128)} %param.6) | copy-start | bytes 1572868
  3.4 1.0 %copy-start.2 = (f32[64,16,128]{2,1,0:T(8,128)S(1)}, f32[64,16,128]{2,1,0:T(8,128)}, u32[]{:S(2)}) copy-start(f32[64,16,128]{2,1,0:T(8,128)} %param.7) | copy-start | bytes 1572868
  4.4 1.0 %copy-start.3 = (s32[64,16,128]{2,1,0:T(8,128)S(1)}, s32[64,16,128]{2,1,0:T(8,128)}, u32[]{:S(2)}) copy-start(s32[64,16,128]{2,1,0:T(8,128)} %param.9) | copy-start | bytes 1572868

commit v2 on v1

--- a/solution.py
+++ b/solution.py
@@ -42,13 +42,13 @@
 
 def kernel(
     count_line, count_chip, count_layer,
-    temp_hbm, power_hbm, weight_hbm, lut, label_hbm,
-    res_hbm, heat_hbm,
-    temp, power, weight, label, cond, res, heat,
+    temp_hbm, power_hbm, weight_hbm, lut_hbm, label_hbm,
+    res, heat,
+    temp, power, weight, label, lut, cond,
     gx, coef_t, coef_u, coef_q,
     line_send, line_recv, layer_send, layer_recv, chip_send, chip_recv,
     mats, rights,
-    in_sem, out_sem, halo_send_sem, halo_recv_sem,
+    in_sem, halo_send_sem, halo_recv_sem,
     mat_send_sem, mat_recv_sem, rhs_send_sem, rhs_recv_sem,
 ):
     line = lax.axis_index("line")
@@ -59,11 +59,14 @@
     loads = [
         pltpu.make_async_copy(src, dst, in_sem.at[n])
         for n, (src, dst) in enumerate(
-            ((label_hbm, label), (temp_hbm, temp), (power_hbm, power), (weight_hbm, weight))
+            (
+                (label_hbm, label), (temp_hbm, temp), (power_hbm, power),
+                (weight_hbm, weight), (lut_hbm, lut),
+            )
         )
     ]
-    for load in loads:
-        load.start()
+    for n in (4, 0, 1, 2, 3):
+        loads[n].start()
 
     line_recv[...] = jnp.zeros_like(line_recv)
     layer_recv[...] = jnp.zeros_like(layer_recv)
@@ -118,6 +121,7 @@
                 device_id_type=MESH,
             ).wait_recv()
 
+    loads[4].wait()
     values = [lut[n] for n in range(8)]
     loads[0].wait()
 
@@ -315,8 +319,6 @@
             held = coef_t[:, i - 1] * rb
             coef_q[:, i - 1] = coef_q[:, i - 1] * rb
             rb = right + held
-    res_copy = pltpu.make_async_copy(res, res_hbm, out_sem.at[0])
-    res_copy.start()
 
     held = []
     for (u1, t1, inv1), (u2, t2, inv2) in tree:
@@ -396,8 +398,6 @@
     for i in range(STEPS - 2, 0, -1):
         x = coef_q[:, i] + coef_u[:, i] * xa + coef_t[:, i] * x
         heat[:, i] = weight[:, i] * x
-    heat_copy = pltpu.make_async_copy(heat, heat_hbm, out_sem.at[1])
-    heat_copy.start()
 
     for side in range(6):
         @pl.when(has[side])
@@ -405,8 +405,17 @@
             halo(side).wait_send()
     for copy in mat_copies + rhs_copies:
         copy.wait_send()
-    res_copy.wait()
-    heat_copy.wait()
+
+
+def store(res, heat, res_hbm, heat_hbm, sem):
+    copies = [
+        pltpu.make_async_copy(res, res_hbm, sem.at[0]),
+        pltpu.make_async_copy(heat, heat_hbm, sem.at[1]),
+    ]
+    for copy in copies:
+        copy.start()
+    for copy in copies:
+        copy.wait()
 
 
 def shards(counts, warmth_field, power_input, inertia_weight, conductivity_lookup, substance_label):
@@ -416,30 +425,47 @@
     whole = vmem(shape, F32)
     others = counts[0] - 1
     dma = pltpu.SemaphoreType.DMA
-    any_space = pl.BlockSpec(memory_space=pl.ANY)
+    hbm_space = pl.BlockSpec(memory_space=pltpu.HBM)
+    vmem_space = pl.BlockSpec(memory_space=pltpu.VMEM)
     flat = (RUNS * STEPS * depth, width)
     rows = vmem(flat, F32)
     residual, heat_rate = pl.pallas_call(
         functools.partial(kernel, *counts),
-        out_shape=(jax.ShapeDtypeStruct(flat, F32), jax.ShapeDtypeStruct(shape, F32)),
-        in_specs=[any_space, any_space, any_space, pl.BlockSpec(memory_space=pltpu.SMEM), any_space],
-        out_specs=(any_space, any_space),
+        out_shape=(rows, whole),
+        in_specs=[hbm_space] * 5,
+        out_specs=(vmem_space, vmem_space),
         scratch_shapes=[
-            rows, whole, whole, vmem(shape, jnp.int32), rows, rows, whole,
+            rows, whole, whole, vmem(shape, jnp.int32), pltpu.SMEM((8,), F32), rows,
             whole, whole, whole, whole,
             vmem((2, 2, depth, width), F32), vmem((2, 2, depth, width), F32),
             vmem((2, 2, RUNS * STEPS, width), F32), vmem((2, 2, RUNS * STEPS, width), F32),
             vmem((2, depth, width), F32), vmem((2, 2, depth, width), F32),
             vmem((counts[0], 4, depth, width), F32), vmem((counts[0], 2, depth, width), F32),
-            dma((4,)), dma((2,)), dma((6,)), dma((6,)),
+            dma((5,)), dma((6,)), dma((6,)),
             dma((others,)), dma((others,)), dma((others,)), dma((others,)),
         ],
         compiler_params=pltpu.CompilerParams(
             collective_id=0, has_side_effects=True, vmem_limit_bytes=32 * 1024 * 1024
         ),
     )(
-        warmth_field.reshape(flat), power_input.reshape(shape), inertia_weight.reshape(shape),
-        conductivity_lookup, substance_label.reshape(shape),
+        *(
+            pltpu.with_memory_space_constraint(operand, pltpu.HBM)
+            for operand in (
+                warmth_field.reshape(flat), power_input.reshape(shape),
+                inertia_weight.reshape(shape), conductivity_lookup,
+                substance_label.reshape(shape),
+            )
+        )
+    )
+    residual, heat_rate = pl.pallas_call(
+        store,
+        out_shape=(jax.ShapeDtypeStruct(flat, F32), jax.ShapeDtypeStruct(shape, F32)),
+        in_specs=[pl.BlockSpec(memory_space=pl.ANY)] * 2,
+        out_specs=(hbm_space, hbm_space),
+        scratch_shapes=[dma((2,))],
+    )(
+        pltpu.with_memory_space_constraint(residual, pltpu.VMEM),
+        pltpu.with_memory_space_constraint(heat_rate, pltpu.VMEM),
     )
     return residual.reshape(warmth_field.shape), heat_rate.reshape(warmth_field.shape)
 

time: 27.3 us -> 21 us (0.77)
  local copies, waits for them, and re-layouts: 6.4 us -> 0 us
  Pallas kernels: 19.9 us -> 20.2 us
    unnamed x12 -> x0, local copies, waits for them, and re-layouts: 6.4 us -> none
    pallas_call x1 -> x2, Pallas kernels: 19.9 us -> 20.2 us  [the longest x1 19.2 us: shards(): pl.pallas_call(functools.partial(kernel, *counts), out_shape=(rows, whole...]
where the time goes in v2:
time: 21 us; the launch traced here: 20.8 us
  Pallas kernels  20.2 us (96%)
  between operations  0.64 us (3%)
    pallas_call x1, Pallas kernels, shards(): pl.pallas_call(functools.partial(kernel, *counts), out_shape=(rows, whole...  19.2 us
    pallas_call x1, Pallas kernels, shards(): pl.pallas_call(store, out_shape=(jax.ShapeDtypeStruct(flat, F32), jax.Sha...  0.99 us

profile of v2, /device:TPU:1, one launch (start us, length us, event | category | flops | bytes accessed | tf_op | source)
XLA Modules:
  0.0 20.8 jit_solution(5991977595247875003)
XLA Ops:
  0.6 19.2 %shard_map.68 = (f32[1024,128]{1,0:T(8,128)S(1)}, f32[8,8,16,128]{3,2,1,0:T(8,128)S(1)}) custom-call(f32[1024,128]{1,0:T(8,128)} %bitcast.6, f32[8,8,16,128]{3,2,1,0:T(8,128)} %bitcast.7, f32[8,8,16,128]{3,2,1,0:T(8,128)} %bitcast.8, f32[8]{0:T(128)} %lut_hbm.1, s32[8,8,16,128]{3,2,1,0:T(8,128)} %bitcast.9), custom_call_target="tpu_custom_call" | custom-call | tf_op jit(solution)/shard_map/pallas_call | solution.py:432
  19.8 1.0 %shard_map.69 = (f32[1024,128]{1,0:T(8,128)}, f32[8,8,16,128]{3,2,1,0:T(8,128)}) custom-call(f32[1024,128]{1,0:T(8,128)S(1)} %get-tuple-element.6.res, f32[8,8,16,128]{3,2,1,0:T(8,128)S(1)} %get-tuple-element.7.heat), custom_call_target="tpu_custom_call" | custom-call | tf_op jit(solution)/shard_map/pallas_call | solution.py:460

commit v3 on v2

v3 whole, which is shorter than its diff:
```python
import functools

import jax
import jax.numpy as jnp
from jax import lax
from jax.experimental import pallas as pl
from jax.experimental.pallas import tpu as pltpu
from jax.sharding import PartitionSpec as P

MESH = pl.DeviceIdType.MESH
RUNS = 8
STEPS = 8
F32 = jnp.float32


def recip(x):
    y = pltpu.reciprocal(x, approx=True)
    return y * (2.0 - x * y)


def conductance(first, second):
    return 2.0 * first * second * recip(first + second)


def eliminate(left, ground, right):
    inv = recip(left + ground + right)
    return left * inv, right * inv, inv


def spot(run, step):
    return pl.ds((run * STEPS + step) * 16, 16)


def read(ref, step):
    return jnp.stack([ref[spot(run, step), :] for run in range(RUNS)])


def write(ref, step, value):
    for run in range(RUNS):
        ref[spot(run, step), :] = value[run]


def kernel(
    count_line, count_chip, count_layer,
    temp_hbm, power_hbm, weight_hbm, lut_hbm, label_hbm,
    res, heat,
    temp, power, weight, label, lut, cond,
    gx, coef_t, coef_u, coef_q,
    line_send, line_recv, layer_send, layer_recv, chip_send, chip_recv,
    mats, rights,
    in_sem, halo_send_sem, halo_recv_sem,
    mat_send_sem, mat_recv_sem, rhs_send_sem, rhs_recv_sem,
):
    line = lax.axis_index("line")
    chip = lax.axis_index("chip")
    layer = lax.axis_index("layer")
    depth, width = 16, 128
    rows = RUNS * STEPS

    has = (
        line > 0, line < count_line - 1,
        layer > 0, layer < count_layer - 1,
        chip > 0, chip < count_chip - 1,
    )
    where = (
        {"line": line - 1}, {"line": line + 1},
        {"layer": layer - 1}, {"layer": layer + 1},
        {"chip": chip - 1}, {"chip": chip + 1},
    )
    sends = (line_send, line_send, layer_send, layer_send, chip_send, chip_send)
    recvs = (line_recv, line_recv, layer_recv, layer_recv, chip_recv, chip_recv)

    other = line + 1 - 2 * lax.rem(line, 2)
    offsets = [4, 2, count_line - 2]
    peers = [lax.rem(core + step, count_line) for step in offsets for core in (line, other)] + [other]
    sources = [peers[n] for n in (0, 1, 4, 5, 2, 3, 6)]

    barrier = pltpu.get_barrier_semaphore()
    for side in range(2, 6):
        @pl.when(has[side])
        def _():
            pl.semaphore_signal(barrier, inc=1, device_id=where[side], device_id_type=MESH)
    for peer in peers[2:] + peers[:2]:
        pl.semaphore_signal(barrier, inc=1, device_id={"line": peer}, device_id_type=MESH)

    loads = [
        pltpu.make_async_copy(src, dst, in_sem.at[n])
        for n, (src, dst) in enumerate(
            (
                (label_hbm, label), (temp_hbm, temp), (lut_hbm, lut),
                (weight_hbm, weight), (power_hbm, power),
            )
        )
    ]
    for load in loads:
        load.start()

    for side in range(6):
        @pl.when(jnp.logical_not(has[side]))
        def _():
            recvs[side][side % 2] = jnp.zeros(recvs[side].shape[1:], F32)

    def halo(side):
        return pltpu.make_async_remote_copy(
            src_ref=sends[side] if side >= 4 else sends[side].at[side % 2],
            dst_ref=recvs[side].at[1 - side % 2],
            send_sem=halo_send_sem.at[side],
            recv_sem=halo_recv_sem.at[side - side % 2 + 1 - side % 2],
            device_id=where[side],
            device_id_type=MESH,
        )

    def halo_start(side):
        @pl.when(has[side])
        def _():
            halo(side).start()

    def halo_landed(side):
        @pl.when(has[side])
        def _():
            pltpu.make_async_remote_copy(
                src_ref=sends[side] if side >= 4 else sends[side].at[side % 2],
                dst_ref=recvs[side].at[side % 2],
                send_sem=halo_send_sem.at[side],
                recv_sem=halo_recv_sem.at[side],
                device_id=where[side],
                device_id_type=MESH,
            ).wait_recv()

    loads[0].wait()
    loads[1].wait()
    start, stop = spot(0, 0), spot(RUNS - 1, STEPS - 1)
    for end, face in ((0, start), (1, stop)):
        line_send[end, 0] = temp[face, :]
        line_send[end, 1] = label[face, :].astype(F32)
    for end, first in ((0, 0), (1, depth - 1)):
        face = pl.ds(first, rows, stride=depth)
        layer_send[end, 0] = temp[face, :]
        layer_send[end, 1] = label[face, :].astype(F32)

    lane = lax.broadcasted_iota(jnp.int32, (1, 1, width), 2)
    packed = jnp.zeros((RUNS, depth, width), F32)
    for i in range(STEPS):
        packed = jnp.where(
            lane // 2 == 2 * i, pltpu.roll(read(temp, i), 4 * i + 1, 2),
            jnp.where(
                lane // 2 == 2 * i + 1,
                pltpu.roll(read(label, i).astype(F32), 4 * i + 3, 2),
                packed,
            ),
        )
    packed = packed.reshape(2, 4, depth, width)
    dense = packed[:, 0]
    for k in range(1, 4):
        dense = jnp.where(lane // 32 == k, pltpu.roll(packed[:, k], 32 * k, 2), dense)
    chip_send[...] = dense

    total = count_line - 1 + sum(side.astype(jnp.int32) for side in has[2:])
    pl.semaphore_wait(barrier, total)
    for side in (4, 5, 2, 3, 0, 1):
        halo_start(side)

    loads[2].wait()
    values = [lut[n] for n in range(8)]

    def look_up(tags):
        odd = (tags & 1) == 1
        two = (tags & 2) == 2
        four = tags >= 4
        pairs = [jnp.where(odd, values[2 * n + 1], values[2 * n]) for n in range(4)]
        halves = [jnp.where(two, pairs[2 * n + 1], pairs[2 * n]) for n in range(2)]
        return jnp.where(four, halves[1], halves[0])

    def face_look_up(tags):
        return look_up(tags.astype(jnp.int32))

    for i in range(STEPS):
        write(cond, i, look_up(read(label, i)))

    for i in range(STEPS - 1):
        gx[:, i] = conductance(read(cond, i), read(cond, i + 1))
    k_last, k_first = read(cond, STEPS - 1), read(cond, 0)
    join = conductance(k_last, jnp.concatenate([k_first[1:], k_first[:1]], axis=0))
    gx[:, STEPS - 1] = join

    loads[3].wait()
    ya, c, yb = weight[:, 0], gx[:, 0], weight[:, 1]
    for i in range(1, STEPS - 1):
        u, t, inv = eliminate(c, yb, gx[:, i])
        ya = ya + u * yb
        c = c * t
        yb = weight[:, i + 1] + t * yb
        coef_u[:, i] = u
        coef_t[:, i] = t
        coef_q[:, i] = inv
    tree = []
    while ya.shape[0] > 1:
        half = ya.shape[0] // 2
        ya_l, ya_r = (ya.reshape(half, 2, depth, width)[:, n] for n in range(2))
        yb_l, yb_r = (yb.reshape(half, 2, depth, width)[:, n] for n in range(2))
        c_l, c_r = (c.reshape(half, 2, depth, width)[:, n] for n in range(2))
        g, join = (join.reshape(half, 2, depth, width)[:, n] for n in range(2))
        first = eliminate(c_l, yb_l, g)
        u, t, _ = first
        ya = ya_l + u * yb_l
        c = c_l * t
        mid = ya_r + t * yb_l
        second = eliminate(c, mid, c_r)
        u, t, _ = second
        ya = ya + u * mid
        c = c * t
        yb = yb_r + t * mid
        tree.append((first, second))
    ya, c, yb = ya[0], c[0], yb[0]
    t_a, u_a, inv_a = eliminate(2.0 * k_first[0], ya, c)
    y_left, yb, c = t_a * ya, yb + u_a * ya, t_a * c
    u_b, t_b, inv_b = eliminate(c, yb, 2.0 * k_last[RUNS - 1])
    y_left, y_right, c = y_left + u_b * yb, t_b * yb, c * t_b
    mats[line, 0] = y_left
    mats[line, 1] = c
    mats[line, 2] = y_right

    def spread(block, send_sem, recv_sem):
        return [
            pltpu.make_async_remote_copy(
                src_ref=block.at[line],
                dst_ref=block.at[line],
                send_sem=send_sem.at[n],
                recv_sem=recv_sem.at[n],
                device_id={"line": peer},
                device_id_type=MESH,
            )
            for n, peer in enumerate(peers)
        ]

    def landed(block, send_sem, recv_sem):
        for n, source in enumerate(sources):
            pltpu.make_async_remote_copy(
                src_ref=block.at[source],
                dst_ref=block.at[source],
                send_sem=send_sem.at[n],
                recv_sem=recv_sem.at[n],
                device_id={"line": source},
                device_id_type=MESH,
            ).wait_recv()

    mat_copies = spread(mats, mat_send_sem, mat_recv_sem)
    for copy in mat_copies:
        copy.start()

    loads[4].wait()
    row = lax.broadcasted_iota(jnp.int32, (1, depth, 1), 1)
    flow = None
    for i in range(STEPS):
        heat_here, k_here = read(temp, i), read(cond, i)
        flow_y = jnp.where(
            lane == width - 1, 0.0,
            conductance(k_here, pltpu.roll(k_here, width - 1, 2))
            * (heat_here - pltpu.roll(heat_here, width - 1, 2)),
        )
        flow_z = jnp.where(
            row == depth - 1, 0.0,
            conductance(k_here, pltpu.roll(k_here, depth - 1, 1))
            * (heat_here - pltpu.roll(heat_here, depth - 1, 1)),
        )
        part = (
            power[:, i]
            - (flow_y - pltpu.roll(flow_y, 1, 2))
            - (flow_z - pltpu.roll(flow_z, 1, 1))
        )
        if i < STEPS - 1:
            flow_on = gx[:, i] * (heat_here - read(temp, i + 1))
        else:
            flow_on = gx[:-1, i] * (heat_here[:-1] - read(temp, 0)[1:])
            flow_on = jnp.concatenate([flow_on, jnp.zeros((1, depth, width), F32)], axis=0)
        if i > 0:
            part = part + flow
        write(res, i, part - flow_on)
        flow = flow_on
    for run in range(1, RUNS):
        here = spot(run, 0)
        res[here, :] = res[here, :] + flow[run - 1]

    halo_landed(0)
    halo_landed(1)
    for end, face in ((0, start), (1, stop)):
        g = conductance(cond[face, :], face_look_up(line_recv[end, 1]))
        g = jnp.where(has[end], g, 0.0)
        res[face, :] = res[face, :] - g * (temp[face, :] - line_recv[end, 0])
    halo_landed(2)
    halo_landed(3)
    is_top = layer == count_layer - 1
    for end, first in ((0, 0), (1, depth - 1)):
        face = pl.ds(first, rows, stride=depth)
        own_k = cond[face, :]
        g = conductance(own_k, face_look_up(layer_recv[end, 1]))
        if end == 0:
            g = jnp.where(has[2], g, 0.0)
        else:
            g = jnp.where(is_top, own_k, g)
        res[face, :] = res[face, :] - g * (layer_send[end, 0] - layer_recv[end, 0])

    own = chip_send[...]
    own_k = face_look_up(pltpu.roll(own, width - 2, 2))
    halo_landed(4)
    halo_landed(5)
    beside = jnp.where(
        lane % 2 == 0, pltpu.roll(chip_recv[1], width - 1, 2), pltpu.roll(chip_recv[0], 1, 2)
    )
    beside_k = face_look_up(pltpu.roll(beside, width - 2, 2))
    open_lane = ((lane % 4 == 0) & has[5]) | ((lane % 4 == 1) & has[4])
    edge = jnp.where(open_lane, conductance(own_k, beside_k) * (own - beside), 0.0)
    edges = jnp.stack(
        [edge] + [pltpu.roll(edge, width - 32 * k, 2) for k in range(1, 4)], axis=1
    ).reshape(RUNS, depth, width)
    at_edge = (lane == 0) | (lane == width - 1)
    for i in range(STEPS):
        total_res = read(res, i) - jnp.where(
            at_edge, pltpu.roll(edges, width - 1 - 4 * i, 2), 0.0
        )
        write(res, i, total_res)
        right = total_res.astype(jnp.bfloat16).astype(F32)
        if i == 0:
            ra = right
        elif i == 1:
            rb = right
        else:
            ra = ra + coef_u[:, i - 1] * rb
            held = coef_t[:, i - 1] * rb
            coef_q[:, i - 1] = coef_q[:, i - 1] * rb
            rb = right + held

    held = []
    for (u1, t1, inv1), (u2, t2, inv2) in tree:
        half = ra.shape[0] // 2
        ra_l, ra_r = (ra.reshape(half, 2, depth, width)[:, n] for n in range(2))
        rb_l, rb_r = (rb.reshape(half, 2, depth, width)[:, n] for n in range(2))
        mid = ra_r + t1 * rb_l
        held.append((inv1 * rb_l, inv2 * mid))
        ra = ra_l + u1 * rb_l + u2 * mid
        rb = rb_r + t2 * mid
    ra, rb = ra[0], rb[0]
    rb = rb + u_a * ra
    r_left, r_right = t_a * ra + u_b * rb, t_b * rb
    rights[line, 0] = r_left
    rights[line, 1] = r_right
    rhs_copies = spread(rights, rhs_send_sem, rhs_recv_sem)
    for copy in rhs_copies:
        copy.start()
    q_a, q_b = inv_a * ra, inv_b * rb

    landed(mats, mat_send_sem, mat_recv_sem)
    zero = jnp.zeros((depth, width), F32)
    before, after = zero, zero
    up, down = [], []
    for j in range(count_line - 1):
        a = before + mats[j, 0]
        u = mats[j, 1] * recip(a + mats[j, 1])
        before = jnp.where(j < line, mats[j, 2] + u * a, before)
        up.append(u)
        n = count_line - 1 - j
        a = after + mats[n, 2]
        u = mats[n, 1] * recip(a + mats[n, 1])
        after = jnp.where(n > line, mats[n, 0] + u * a, after)
        down.append(u)
    a = y_left + before
    b = y_right + after
    inv = recip(a * b + c * (a + b))
    from_a, from_b, cross = (b + c) * inv, (a + c) * inv, c * inv

    landed(rights, rhs_send_sem, rhs_recv_sem)
    left_in, right_in = zero, zero
    for j in range(count_line - 1):
        new = rights[j, 1] + up[j] * (rights[j, 0] + left_in)
        left_in = jnp.where(j < line, new, left_in)
        n = count_line - 1 - j
        new = rights[n, 0] + down[j] * (rights[n, 1] + right_in)
        right_in = jnp.where(n > line, new, right_in)
    left_in = left_in + r_left
    right_in = right_in + r_right
    x_left = from_a * left_in + cross * right_in
    x_right = cross * left_in + from_b * right_in
    xb = q_b + u_b * x_left + t_b * x_right
    xa = q_a + t_a * x_left + u_a * xb
    xa, xb = xa[None], xb[None]

    for ((u1, t1, _), (u2, t2, _)), (q1, q2) in zip(reversed(tree), reversed(held)):
        xr = q2 + u2 * xa + t2 * xb
        xl = q1 + u1 * xa + t1 * xr
        size = 2 * xa.shape[0]
        xa = jnp.stack([xa, xr], axis=1).reshape(size, depth, width)
        xb = jnp.stack([xl, xb], axis=1).reshape(size, depth, width)
    heat[:, 0] = weight[:, 0] * xa
    heat[:, STEPS - 1] = weight[:, STEPS - 1] * xb
    x = xb
    for i in range(STEPS - 2, 0, -1):
        x = coef_q[:, i] + coef_u[:, i] * xa + coef_t[:, i] * x
        heat[:, i] = weight[:, i] * x

    for side in range(6):
        @pl.when(has[side])
        def _():
            halo(side).wait_send()
    for copy in mat_copies + rhs_copies:
        copy.wait_send()


def store(res, heat, res_hbm, heat_hbm, sem):
    copies = [
        pltpu.make_async_copy(res, res_hbm, sem.at[0]),
        pltpu.make_async_copy(heat, heat_hbm, sem.at[1]),
    ]
    for copy in copies:
        copy.start()
    for copy in copies:
        copy.wait()


def shards(counts, warmth_field, power_input, inertia_weight, conductivity_lookup, substance_label):
    depth, width = warmth_field.shape[1:]
    shape = (RUNS, STEPS, depth, width)
    vmem = pltpu.VMEM
    whole = vmem(shape, F32)
    others = counts[0] - 1
    dma = pltpu.SemaphoreType.DMA
    hbm_space = pl.BlockSpec(memory_space=pltpu.HBM)
    vmem_space = pl.BlockSpec(memory_space=pltpu.VMEM)
    flat = (RUNS * STEPS * depth, width)
    rows = vmem(flat, F32)
    residual, heat_rate = pl.pallas_call(
        functools.partial(kernel, *counts),
        out_shape=(rows, whole),
        in_specs=[hbm_space] * 5,
        out_specs=(vmem_space, vmem_space),
        scratch_shapes=[
            rows, whole, whole, vmem(flat, jnp.int32), pltpu.SMEM((8,), F32), rows,
            whole, whole, whole, whole,
            vmem((2, 2, depth, width), F32), vmem((2, 2, depth, width), F32),
            vmem((2, 2, RUNS * STEPS, width), F32), vmem((2, 2, RUNS * STEPS, width), F32),
            vmem((2, depth, width), F32), vmem((2, 2, depth, width), F32),
            vmem((counts[0], 3, depth, width), F32), vmem((counts[0], 2, depth, width), F32),
            dma((5,)), dma((6,)), dma((6,)),
            dma((others,)), dma((others,)), dma((others,)), dma((others,)),
        ],
        compiler_params=pltpu.CompilerParams(
            collective_id=0, has_side_effects=True, vmem_limit_bytes=32 * 1024 * 1024
        ),
    )(
        *(
            pltpu.with_memory_space_constraint(operand, pltpu.HBM)
            for operand in (
                warmth_field.reshape(flat), power_input.reshape(shape),
                inertia_weight.reshape(shape), conductivity_lookup,
                substance_label.reshape(flat),
            )
        )
    )
    residual, heat_rate = pl.pallas_call(
        store,
        out_shape=(jax.ShapeDtypeStruct(flat, F32), jax.ShapeDtypeStruct(shape, F32)),
        in_specs=[pl.BlockSpec(memory_space=pl.ANY)] * 2,
        out_specs=(hbm_space, hbm_space),
        scratch_shapes=[dma((2,))],
    )(
        pltpu.with_memory_space_constraint(residual, pltpu.VMEM),
        pltpu.with_memory_space_constraint(heat_rate, pltpu.VMEM),
    )
    return residual.reshape(warmth_field.shape), heat_rate.reshape(warmth_field.shape)


def solution(mesh):
    counts = tuple(mesh.shape[axis] for axis in ("line", "chip", "layer"))
    spec = P("line", "layer", "chip")
    return jax.shard_map(
        functools.partial(shards, counts),
        mesh=mesh,
        in_specs=(spec, spec, spec, P(), spec),
        out_specs=(spec, spec),
        check_vma=False,
    )
```

time: 21 us -> 18 us (0.86)
  Pallas kernels: 20.2 us -> 17.2 us
    pallas_call x1, Pallas kernels: 19.2 us -> 16.3 us  [shards(): pl.pallas_call(functools.partial(kernel, *counts), out_shape=(rows, whole...]
where the time goes in v3:
time: 18 us; the launch traced here: 17.9 us
  Pallas kernels  17.2 us (96%)
  between operations  0.64 us (4%)
    pallas_call x1, Pallas kernels, shards(): pl.pallas_call(functools.partial(kernel, *counts), out_shape=(rows, whole...  16.3 us
    pallas_call x1, Pallas kernels, shards(): pl.pallas_call(store, out_shape=(jax.ShapeDtypeStruct(flat, F32), jax.Sha...  0.99 us

profile of v3, /device:TPU:1, one launch (start us, length us, event | category | flops | bytes accessed | tf_op | source)
XLA Modules:
  0.0 17.9 jit_solution(2157007849960917307)
XLA Ops:
  0.6 16.3 %shard_map.68 = (f32[1024,128]{1,0:T(8,128)S(1)}, f32[8,8,16,128]{3,2,1,0:T(8,128)S(1)}) custom-call(f32[1024,128]{1,0:T(8,128)} %bitcast.6, f32[8,8,16,128]{3,2,1,0:T(8,128)} %bitcast.7, f32[8,8,16,128]{3,2,1,0:T(8,128)} %bitcast.8, f32[8]{0:T(128)} %lut_hbm.1, s32[1024,128]{1,0:T(8,128)} %bitcast.9), custom_call_target="tpu_custom_call" | custom-call | tf_op jit(solution)/shard_map/pallas_call | solution.py:430
  16.9 1.0 %shard_map.69 = (f32[1024,128]{1,0:T(8,128)}, f32[8,8,16,128]{3,2,1,0:T(8,128)}) custom-call(f32[1024,128]{1,0:T(8,128)S(1)} %get-tuple-element.6.res, f32[8,8,16,128]{3,2,1,0:T(8,128)S(1)} %get-tuple-element.7.heat), custom_call_target="tpu_custom_call" | custom-call | tf_op jit(solution)/shard_map/pallas_call | solution.py:458

commit v4 on v3

--- a/solution.py
+++ b/solution.py
@@ -49,7 +49,7 @@
     line_send, line_recv, layer_send, layer_recv, chip_send, chip_recv,
     mats, rights,
     in_sem, halo_send_sem, halo_recv_sem,
-    mat_send_sem, mat_recv_sem, rhs_send_sem, rhs_recv_sem,
+    mat_send_sem, mat_recv_sem, rhs_send_sem, rhs_recv_sem, ready_sem,
 ):
     line = lax.axis_index("line")
     chip = lax.axis_index("chip")
@@ -80,8 +80,11 @@
         @pl.when(has[side])
         def _():
             pl.semaphore_signal(barrier, inc=1, device_id=where[side], device_id_type=MESH)
-    for peer in peers[2:] + peers[:2]:
-        pl.semaphore_signal(barrier, inc=1, device_id={"line": peer}, device_id_type=MESH)
+    greets = [((line > 0) & (peer > 0)) | (line + peer == 1) for peer in peers]
+    for n in (6, 2, 3, 4, 5, 0, 1):
+        @pl.when(greets[n])
+        def _():
+            pl.semaphore_signal(barrier, inc=1, device_id={"line": peers[n]}, device_id_type=MESH)
 
     loads = [
         pltpu.make_async_copy(src, dst, in_sem.at[n])
@@ -155,10 +158,14 @@
         dense = jnp.where(lane // 32 == k, pltpu.roll(packed[:, k], 32 * k, 2), dense)
     chip_send[...] = dense
 
-    total = count_line - 1 + sum(side.astype(jnp.int32) for side in has[2:])
-    pl.semaphore_wait(barrier, total)
+    pl.semaphore_wait(barrier, sum(met.astype(jnp.int32) for met in greets + list(has[2:])))
     for side in (4, 5, 2, 3, 0, 1):
         halo_start(side)
+
+    @pl.when(line == 1)
+    def _():
+        for peer in [peers[n] for n in (6, 0, 1, 2, 3, 4, 5)]:
+            pl.semaphore_signal(ready_sem, inc=1, device_id={"line": peer}, device_id_type=MESH)
 
     loads[2].wait()
     values = [lut[n] for n in range(8)]
@@ -245,8 +252,24 @@
             ).wait_recv()
 
     mat_copies = spread(mats, mat_send_sem, mat_recv_sem)
-    for copy in mat_copies:
-        copy.start()
+
+    @pl.when(line == 0)
+    def _():
+        pl.semaphore_wait(ready_sem, 1)
+
+    def start_others(copies):
+        for peer, copy in zip(peers, copies):
+            @pl.when(peer > 0)
+            def _():
+                copy.start()
+
+    def start_first(copies):
+        for peer, copy in zip(peers, copies):
+            @pl.when(peer == 0)
+            def _():
+                copy.start()
+
+    start_others(mat_copies)
 
     loads[4].wait()
     row = lax.broadcasted_iota(jnp.int32, (1, depth, 1), 1)
@@ -345,8 +368,14 @@
     rights[line, 0] = r_left
     rights[line, 1] = r_right
     rhs_copies = spread(rights, rhs_send_sem, rhs_recv_sem)
-    for copy in rhs_copies:
-        copy.start()
+    start_others(rhs_copies)
+
+    @pl.when(line > 1)
+    def _():
+        pl.semaphore_wait(ready_sem, 1)
+
+    start_first(mat_copies)
+    start_first(rhs_copies)
     q_a, q_b = inv_a * ra, inv_b * rb
 
     landed(mats, mat_send_sem, mat_recv_sem)
@@ -441,6 +470,7 @@
             vmem((counts[0], 3, depth, width), F32), vmem((counts[0], 2, depth, width), F32),
             dma((5,)), dma((6,)), dma((6,)),
             dma((others,)), dma((others,)), dma((others,)), dma((others,)),
+            pltpu.SemaphoreType.REGULAR,
         ],
         compiler_params=pltpu.CompilerParams(
             collective_id=0, has_side_effects=True, vmem_limit_bytes=32 * 1024 * 1024

time: 18 us -> 16.3 us (0.906)
  the two profiles are of different devices: /device:TPU:1 before, /device:TPU:11 now
where the time goes in v4:
time: 16.3 us; the launch traced here: 16.2 us
  Pallas kernels  15.5 us (95%)
  between operations  0.64 us (4%)
    pallas_call x1, Pallas kernels, shards(): pl.pallas_call(functools.partial(kernel, *counts), out_shape=(rows, whole...  14.5 us
    pallas_call x1, Pallas kernels, shards(): pl.pallas_call(store, out_shape=(jax.ShapeDtypeStruct(flat, F32), jax.Sha...  0.99 us

profile of v4, /device:TPU:11, one launch (start us, length us, event | category | flops | bytes accessed | tf_op | source)
XLA Modules:
  0.0 16.2 jit_solution(13324470730776882705)
XLA Ops:
  0.6 14.5 %shard_map.68 = (f32[1024,128]{1,0:T(8,128)S(1)}, f32[8,8,16,128]{3,2,1,0:T(8,128)S(1)}) custom-call(f32[1024,128]{1,0:T(8,128)} %bitcast.6, f32[8,8,16,128]{3,2,1,0:T(8,128)} %bitcast.7, f32[8,8,16,128]{3,2,1,0:T(8,128)} %bitcast.8, f32[8]{0:T(128)} %lut_hbm.1, s32[1024,128]{1,0:T(8,128)} %bitcast.9), custom_call_target="tpu_custom_call" | custom-call | tf_op jit(solution)/shard_map/pallas_call | solution.py:459
  15.2 1.0 %shard_map.69 = (f32[1024,128]{1,0:T(8,128)}, f32[8,8,16,128]{3,2,1,0:T(8,128)}) custom-call(f32[1024,128]{1,0:T(8,128)S(1)} %get-tuple-element.6.res, f32[8,8,16,128]{3,2,1,0:T(8,128)S(1)} %get-tuple-element.7.heat), custom_call_target="tpu_custom_call" | custom-call | tf_op jit(solution)/shard_map/pallas_call | solution.py:488

commit v5 on v4

--- a/solution.py
+++ b/solution.py
@@ -14,8 +14,7 @@
 
 
 def recip(x):
-    y = pltpu.reciprocal(x, approx=True)
-    return y * (2.0 - x * y)
+    return pltpu.reciprocal(x, approx=True)
 
 
 def conductance(first, second):
@@ -27,17 +26,20 @@
     return left * inv, right * inv, inv
 
 
-def spot(run, step):
-    return pl.ds((run * STEPS + step) * 16, 16)
-
-
-def read(ref, step):
-    return jnp.stack([ref[spot(run, step), :] for run in range(RUNS)])
-
-
-def write(ref, step, value):
+PAD = 8
+
+
+def spot(run, step, shift=0):
+    return pl.ds((run * STEPS + step) * 16 + shift, 16)
+
+
+def read(ref, step, shift=0):
+    return jnp.stack([ref[spot(run, step, shift), :] for run in range(RUNS)])
+
+
+def write(ref, step, value, shift=0):
     for run in range(RUNS):
-        ref[spot(run, step), :] = value[run]
+        ref[spot(run, step, shift), :] = value[run]
 
 
 def kernel(
@@ -80,7 +82,9 @@
         @pl.when(has[side])
         def _():
             pl.semaphore_signal(barrier, inc=1, device_id=where[side], device_id_type=MESH)
-    greets = [((line > 0) & (peer > 0)) | (line + peer == 1) for peer in peers]
+    first_lines = (chip == 0) & (layer == 0)
+    other_lines = jnp.logical_not(first_lines)
+    greets = [other_lines | ((line > 0) & (peer > 0)) | (line + peer == 1) for peer in peers]
     for n in (6, 2, 3, 4, 5, 0, 1):
         @pl.when(greets[n])
         def _():
@@ -90,7 +94,7 @@
         pltpu.make_async_copy(src, dst, in_sem.at[n])
         for n, (src, dst) in enumerate(
             (
-                (label_hbm, label), (temp_hbm, temp), (lut_hbm, lut),
+                (label_hbm, label), (temp_hbm, temp.at[pl.ds(PAD, rows * depth)]), (lut_hbm, lut),
                 (weight_hbm, weight), (power_hbm, power),
             )
         )
@@ -130,22 +134,25 @@
                 device_id_type=MESH,
             ).wait_recv()
 
+    for ref in (temp, cond):
+        for first in (0, rows * depth + PAD):
+            ref[pl.ds(first, PAD), :] = jnp.zeros((PAD, width), F32)
+
     loads[0].wait()
     loads[1].wait()
-    start, stop = spot(0, 0), spot(RUNS - 1, STEPS - 1)
-    for end, face in ((0, start), (1, stop)):
-        line_send[end, 0] = temp[face, :]
-        line_send[end, 1] = label[face, :].astype(F32)
-    for end, first in ((0, 0), (1, depth - 1)):
-        face = pl.ds(first, rows, stride=depth)
-        layer_send[end, 0] = temp[face, :]
-        layer_send[end, 1] = label[face, :].astype(F32)
+    x_ends = ((0, 0), (RUNS - 1, STEPS - 1))
+    z_ends = (0, depth - 1)
+    for end in range(2):
+        line_send[end, 0] = temp[spot(*x_ends[end], PAD), :]
+        line_send[end, 1] = label[spot(*x_ends[end]), :].astype(F32)
+        layer_send[end, 0] = temp[pl.ds(z_ends[end] + PAD, rows, stride=depth), :]
+        layer_send[end, 1] = label[pl.ds(z_ends[end], rows, stride=depth), :].astype(F32)
 
     lane = lax.broadcasted_iota(jnp.int32, (1, 1, width), 2)
     packed = jnp.zeros((RUNS, depth, width), F32)
     for i in range(STEPS):
         packed = jnp.where(
-            lane // 2 == 2 * i, pltpu.roll(read(temp, i), 4 * i + 1, 2),
+            lane // 2 == 2 * i, pltpu.roll(read(temp, i, PAD), 4 * i + 1, 2),
             jnp.where(
                 lane // 2 == 2 * i + 1,
                 pltpu.roll(read(label, i).astype(F32), 4 * i + 3, 2),
@@ -159,10 +166,11 @@
     chip_send[...] = dense
 
     pl.semaphore_wait(barrier, sum(met.astype(jnp.int32) for met in greets + list(has[2:])))
-    for side in (4, 5, 2, 3, 0, 1):
+    for side in (2, 3, 4, 5, 0, 1):
         halo_start(side)
 
-    @pl.when(line == 1)
+
+    @pl.when(first_lines & (line == 1))
     def _():
         for peer in [peers[n] for n in (6, 0, 1, 2, 3, 4, 5)]:
             pl.semaphore_signal(ready_sem, inc=1, device_id={"line": peer}, device_id_type=MESH)
@@ -182,11 +190,11 @@
         return look_up(tags.astype(jnp.int32))
 
     for i in range(STEPS):
-        write(cond, i, look_up(read(label, i)))
+        write(cond, i, look_up(read(label, i)), PAD)
 
     for i in range(STEPS - 1):
-        gx[:, i] = conductance(read(cond, i), read(cond, i + 1))
-    k_last, k_first = read(cond, STEPS - 1), read(cond, 0)
+        gx[:, i] = conductance(read(cond, i, PAD), read(cond, i + 1, PAD))
+    k_last, k_first = read(cond, STEPS - 1, PAD), read(cond, 0, PAD)
     join = conductance(k_last, jnp.concatenate([k_first[1:], k_first[:1]], axis=0))
     gx[:, STEPS - 1] = join
 
@@ -253,19 +261,19 @@
 
     mat_copies = spread(mats, mat_send_sem, mat_recv_sem)
 
-    @pl.when(line == 0)
+    @pl.when(first_lines & (line == 0))
     def _():
         pl.semaphore_wait(ready_sem, 1)
 
     def start_others(copies):
         for peer, copy in zip(peers, copies):
-            @pl.when(peer > 0)
+            @pl.when(other_lines | (peer > 0))
             def _():
                 copy.start()
 
     def start_first(copies):
         for peer, copy in zip(peers, copies):
-            @pl.when(peer == 0)
+            @pl.when(first_lines & (peer == 0))
             def _():
                 copy.start()
 
@@ -275,26 +283,21 @@
     row = lax.broadcasted_iota(jnp.int32, (1, depth, 1), 1)
     flow = None
     for i in range(STEPS):
-        heat_here, k_here = read(temp, i), read(cond, i)
+        heat_here, k_here = read(temp, i, PAD), read(cond, i, PAD)
         flow_y = jnp.where(
             lane == width - 1, 0.0,
             conductance(k_here, pltpu.roll(k_here, width - 1, 2))
             * (heat_here - pltpu.roll(heat_here, width - 1, 2)),
         )
-        flow_z = jnp.where(
+        flow_up = jnp.where(
             row == depth - 1, 0.0,
-            conductance(k_here, pltpu.roll(k_here, depth - 1, 1))
-            * (heat_here - pltpu.roll(heat_here, depth - 1, 1)),
+            conductance(k_here, read(cond, i, PAD + 1)) * (heat_here - read(temp, i, PAD + 1)),
         )
-        part = (
-            power[:, i]
-            - (flow_y - pltpu.roll(flow_y, 1, 2))
-            - (flow_z - pltpu.roll(flow_z, 1, 1))
-        )
+        part = power[:, i] - (flow_y - pltpu.roll(flow_y, 1, 2)) - (flow_up - pltpu.roll(flow_up, 1, 1))
         if i < STEPS - 1:
-            flow_on = gx[:, i] * (heat_here - read(temp, i + 1))
+            flow_on = gx[:, i] * (heat_here - read(temp, i + 1, PAD))
         else:
-            flow_on = gx[:-1, i] * (heat_here[:-1] - read(temp, 0)[1:])
+            flow_on = gx[:-1, i] * (heat_here[:-1] - read(temp, 0, PAD)[1:])
             flow_on = jnp.concatenate([flow_on, jnp.zeros((1, depth, width), F32)], axis=0)
         if i > 0:
             part = part + flow
@@ -306,22 +309,11 @@
 
     halo_landed(0)
     halo_landed(1)
-    for end, face in ((0, start), (1, stop)):
-        g = conductance(cond[face, :], face_look_up(line_recv[end, 1]))
+    for end in range(2):
+        here = spot(*x_ends[end])
+        g = conductance(cond[spot(*x_ends[end], PAD), :], face_look_up(line_recv[end, 1]))
         g = jnp.where(has[end], g, 0.0)
-        res[face, :] = res[face, :] - g * (temp[face, :] - line_recv[end, 0])
-    halo_landed(2)
-    halo_landed(3)
-    is_top = layer == count_layer - 1
-    for end, first in ((0, 0), (1, depth - 1)):
-        face = pl.ds(first, rows, stride=depth)
-        own_k = cond[face, :]
-        g = conductance(own_k, face_look_up(layer_recv[end, 1]))
-        if end == 0:
-            g = jnp.where(has[2], g, 0.0)
-        else:
-            g = jnp.where(is_top, own_k, g)
-        res[face, :] = res[face, :] - g * (layer_send[end, 0] - layer_recv[end, 0])
+        res[here, :] = res[here, :] - g * (line_send[end, 0] - line_recv[end, 0])
 
     own = chip_send[...]
     own_k = face_look_up(pltpu.roll(own, width - 2, 2))
@@ -338,11 +330,25 @@
     ).reshape(RUNS, depth, width)
     at_edge = (lane == 0) | (lane == width - 1)
     for i in range(STEPS):
-        total_res = read(res, i) - jnp.where(
+        write(res, i, read(res, i) - jnp.where(
             at_edge, pltpu.roll(edges, width - 1 - 4 * i, 2), 0.0
-        )
-        write(res, i, total_res)
-        right = total_res.astype(jnp.bfloat16).astype(F32)
+        ))
+
+    is_top = layer == count_layer - 1
+    own_faces = [cond[pl.ds(first + PAD, rows, stride=depth), :] for first in z_ends]
+    halo_landed(2)
+    halo_landed(3)
+    for end in range(2):
+        face = pl.ds(z_ends[end], rows, stride=depth)
+        own_k = own_faces[end]
+        g = conductance(own_k, face_look_up(layer_recv[end, 1]))
+        if end == 0:
+            g = jnp.where(has[2], g, 0.0)
+        else:
+            g = jnp.where(is_top, own_k, g)
+        res[face, :] = res[face, :] - g * (layer_send[end, 0] - layer_recv[end, 0])
+    for i in range(STEPS):
+        right = read(res, i).astype(jnp.bfloat16).astype(F32)
         if i == 0:
             ra = right
         elif i == 1:
@@ -370,7 +376,7 @@
     rhs_copies = spread(rights, rhs_send_sem, rhs_recv_sem)
     start_others(rhs_copies)
 
-    @pl.when(line > 1)
+    @pl.when(first_lines & (line > 1))
     def _():
         pl.semaphore_wait(ready_sem, 1)
 
@@ -456,13 +462,14 @@
     vmem_space = pl.BlockSpec(memory_space=pltpu.VMEM)
     flat = (RUNS * STEPS * depth, width)
     rows = vmem(flat, F32)
+    padded = vmem((flat[0] + 2 * PAD, width), F32)
     residual, heat_rate = pl.pallas_call(
         functools.partial(kernel, *counts),
         out_shape=(rows, whole),
         in_specs=[hbm_space] * 5,
         out_specs=(vmem_space, vmem_space),
         scratch_shapes=[
-            rows, whole, whole, vmem(flat, jnp.int32), pltpu.SMEM((8,), F32), rows,
+            padded, whole, whole, vmem(flat, jnp.int32), pltpu.SMEM((8,), F32), padded,
             whole, whole, whole, whole,
             vmem((2, 2, depth, width), F32), vmem((2, 2, depth, width), F32),
             vmem((2, 2, RUNS * STEPS, width), F32), vmem((2, 2, RUNS * STEPS, width), F32),

time: 16.3 us -> 16 us (0.982)
  the two profiles are of different devices: /device:TPU:11 before, /device:TPU:1 now
where the time goes in v5:
time: 16 us; the launch traced here: 15.8 us
  Pallas kernels  15.2 us (95%)
  between operations  0.64 us (4%)
    pallas_call x1, Pallas kernels, shards(): pl.pallas_call(functools.partial(kernel, *counts), out_shape=(rows, whole...  14.2 us
    pallas_call x1, Pallas kernels, shards(): pl.pallas_call(store, out_shape=(jax.ShapeDtypeStruct(flat, F32), jax.Sha...  0.99 us

profile of v5, /device:TPU:1, one launch (start us, length us, event | category | flops | bytes accessed | tf_op | source)
XLA Modules:
  0.0 15.8 jit_solution(2636252651838480827)
XLA Ops:
  0.6 14.2 %shard_map.68 = (f32[1024,128]{1,0:T(8,128)S(1)}, f32[8,8,16,128]{3,2,1,0:T(8,128)S(1)}) custom-call(f32[1024,128]{1,0:T(8,128)} %bitcast.6, f32[8,8,16,128]{3,2,1,0:T(8,128)} %bitcast.7, f32[8,8,16,128]{3,2,1,0:T(8,128)} %bitcast.8, f32[8]{0:T(128)} %lut_hbm.1, s32[1024,128]{1,0:T(8,128)} %bitcast.9), custom_call_target="tpu_custom_call" | custom-call | tf_op jit(solution)/shard_map/pallas_call | solution.py:466
  14.8 1.0 %shard_map.69 = (f32[1024,128]{1,0:T(8,128)}, f32[8,8,16,128]{3,2,1,0:T(8,128)}) custom-call(f32[1024,128]{1,0:T(8,128)S(1)} %get-tuple-element.6.res, f32[8,8,16,128]{3,2,1,0:T(8,128)S(1)} %get-tuple-element.7.heat), custom_call_target="tpu_custom_call" | custom-call | tf_op jit(solution)/shard_map/pallas_call | solution.py:495

commit v6 on v5

--- a/solution.py
+++ b/solution.py
@@ -45,9 +45,8 @@
 def kernel(
     count_line, count_chip, count_layer,
     temp_hbm, power_hbm, weight_hbm, lut_hbm, label_hbm,
-    res, heat,
-    temp, power, weight, label, lut, cond,
-    gx, coef_t, coef_u, coef_q,
+    res, weight, coef_t, coef_u, coef_q, run_ends,
+    temp, power, label, lut, cond, gx,
     line_send, line_recv, layer_send, layer_recv, chip_send, chip_recv,
     mats, rights,
     in_sem, halo_send_sem, halo_recv_sem,
@@ -82,14 +81,6 @@
         @pl.when(has[side])
         def _():
             pl.semaphore_signal(barrier, inc=1, device_id=where[side], device_id_type=MESH)
-    first_lines = (chip == 0) & (layer == 0)
-    other_lines = jnp.logical_not(first_lines)
-    greets = [other_lines | ((line > 0) & (peer > 0)) | (line + peer == 1) for peer in peers]
-    for n in (6, 2, 3, 4, 5, 0, 1):
-        @pl.when(greets[n])
-        def _():
-            pl.semaphore_signal(barrier, inc=1, device_id={"line": peers[n]}, device_id_type=MESH)
-
     loads = [
         pltpu.make_async_copy(src, dst, in_sem.at[n])
         for n, (src, dst) in enumerate(
@@ -101,6 +92,15 @@
     ]
     for load in loads:
         load.start()
+
+    first_lines = (chip == 0) & (layer == 0)
+    other_lines = jnp.logical_not(first_lines)
+    greets = [other_lines | ((line > 0) & (peer > 0)) | (line + peer == 1) for peer in peers]
+    for n in (6, 2, 3, 4, 5, 0, 1):
+        @pl.when(greets[n])
+        def _():
+            pl.semaphore_signal(barrier, inc=1, device_id={"line": peers[n]}, device_id_type=MESH)
+
 
     for side in range(6):
         @pl.when(jnp.logical_not(has[side]))
@@ -266,16 +266,31 @@
         pl.semaphore_wait(ready_sem, 1)
 
     def start_others(copies):
-        for peer, copy in zip(peers, copies):
-            @pl.when(other_lines | (peer > 0))
-            def _():
+        @pl.when(other_lines | (line == 0))
+        def _():
+            for copy in copies:
                 copy.start()
 
-    def start_first(copies):
-        for peer, copy in zip(peers, copies):
-            @pl.when(first_lines & (peer == 0))
-            def _():
-                copy.start()
+        @pl.when(first_lines & (line > 0))
+        def _():
+            for peer, copy in zip(peers, copies):
+                @pl.when(peer > 0)
+                def _():
+                    copy.start()
+
+    def start_first(block, send_sem, recv_sem):
+        n = sum(jnp.where(peer == 0, n, 0) for n, peer in enumerate(peers))
+
+        @pl.when(first_lines & (line > 0))
+        def _():
+            pltpu.make_async_remote_copy(
+                src_ref=block.at[line],
+                dst_ref=block.at[line],
+                send_sem=send_sem.at[n],
+                recv_sem=recv_sem.at[n],
+                device_id={"line": 0},
+                device_id_type=MESH,
+            ).start()
 
     start_others(mat_copies)
 
@@ -307,6 +322,12 @@
         here = spot(run, 0)
         res[here, :] = res[here, :] + flow[run - 1]
 
+    @pl.when(first_lines & (line > 1))
+    def _():
+        pl.semaphore_wait(ready_sem, 1)
+
+    start_first(mats, mat_send_sem, mat_recv_sem)
+
     halo_landed(0)
     halo_landed(1)
     for end in range(2):
@@ -376,12 +397,7 @@
     rhs_copies = spread(rights, rhs_send_sem, rhs_recv_sem)
     start_others(rhs_copies)
 
-    @pl.when(first_lines & (line > 1))
-    def _():
-        pl.semaphore_wait(ready_sem, 1)
-
-    start_first(mat_copies)
-    start_first(rhs_copies)
+    start_first(rights, rhs_send_sem, rhs_recv_sem)
     q_a, q_b = inv_a * ra, inv_b * rb
 
     landed(mats, mat_send_sem, mat_recv_sem)
@@ -425,12 +441,8 @@
         size = 2 * xa.shape[0]
         xa = jnp.stack([xa, xr], axis=1).reshape(size, depth, width)
         xb = jnp.stack([xl, xb], axis=1).reshape(size, depth, width)
-    heat[:, 0] = weight[:, 0] * xa
-    heat[:, STEPS - 1] = weight[:, STEPS - 1] * xb
-    x = xb
-    for i in range(STEPS - 2, 0, -1):
-        x = coef_q[:, i] + coef_u[:, i] * xa + coef_t[:, i] * x
-        heat[:, i] = weight[:, i] * x
+    run_ends[0] = xa
+    run_ends[1] = xb
 
     for side in range(6):
         @pl.when(has[side])
@@ -440,13 +452,22 @@
         copy.wait_send()
 
 
-def store(res, heat, res_hbm, heat_hbm, sem):
-    copies = [
-        pltpu.make_async_copy(res, res_hbm, sem.at[0]),
-        pltpu.make_async_copy(heat, heat_hbm, sem.at[1]),
-    ]
-    for copy in copies:
-        copy.start()
+def finish(res, weight, coef_t, coef_u, coef_q, run_ends, res_hbm, heat_hbm, heat, sem):
+    copies = [pltpu.make_async_copy(res, res_hbm, sem.at[2])]
+    copies[0].start()
+    xa, x = run_ends[0], run_ends[1]
+    for i in range(STEPS - 1, -1, -1):
+        if i == 0:
+            x = xa
+        elif i < STEPS - 1:
+            x = coef_q[:, i] + coef_u[:, i] * xa + coef_t[:, i] * x
+        heat[:, i] = weight[:, i] * x
+        if i % 4 == 0:
+            part = pl.ds(i, 4)
+            copies.append(
+                pltpu.make_async_copy(heat.at[:, part], heat_hbm.at[:, part], sem.at[i // 4])
+            )
+            copies[-1].start()
     for copy in copies:
         copy.wait()
 
@@ -463,14 +484,13 @@
     flat = (RUNS * STEPS * depth, width)
     rows = vmem(flat, F32)
     padded = vmem((flat[0] + 2 * PAD, width), F32)
-    residual, heat_rate = pl.pallas_call(
+    held = pl.pallas_call(
         functools.partial(kernel, *counts),
-        out_shape=(rows, whole),
+        out_shape=(rows, whole, whole, whole, whole, vmem((2, RUNS, depth, width), F32)),
         in_specs=[hbm_space] * 5,
-        out_specs=(vmem_space, vmem_space),
+        out_specs=(vmem_space,) * 6,
         scratch_shapes=[
-            padded, whole, whole, vmem(flat, jnp.int32), pltpu.SMEM((8,), F32), padded,
-            whole, whole, whole, whole,
+            padded, whole, vmem(flat, jnp.int32), pltpu.SMEM((8,), F32), padded, whole,
             vmem((2, 2, depth, width), F32), vmem((2, 2, depth, width), F32),
             vmem((2, 2, RUNS * STEPS, width), F32), vmem((2, 2, RUNS * STEPS, width), F32),
             vmem((2, depth, width), F32), vmem((2, 2, depth, width), F32),
@@ -493,15 +513,12 @@
         )
     )
     residual, heat_rate = pl.pallas_call(
-        store,
+        finish,
         out_shape=(jax.ShapeDtypeStruct(flat, F32), jax.ShapeDtypeStruct(shape, F32)),
-        in_specs=[pl.BlockSpec(memory_space=pl.ANY)] * 2,
+        in_specs=[vmem_space] * 6,
         out_specs=(hbm_space, hbm_space),
-        scratch_shapes=[dma((2,))],
-    )(
-        pltpu.with_memory_space_constraint(residual, pltpu.VMEM),
-        pltpu.with_memory_space_constraint(heat_rate, pltpu.VMEM),
-    )
+        scratch_shapes=[whole, dma((3,))],
+    )(*(pltpu.with_memory_space_constraint(array, pltpu.VMEM) for array in held))
     return residual.reshape(warmth_field.shape), heat_rate.reshape(warmth_field.shape)
 
 

time: 16 us -> 16 us (level)
  no operation moved by 1% of the time
where the time goes in v6:
time: 16 us; the launch traced here: 15.9 us
  Pallas kernels  15.2 us (95%)
  between operations  0.64 us (4%)
    pallas_call x1, Pallas kernels, shards(): pl.pallas_call(functools.partial(kernel, *counts), out_shape=(rows, whole...  14.2 us
    pallas_call x1, Pallas kernels, shards(): pl.pallas_call(finish, out_shape=(jax.ShapeDtypeStruct(flat, F32), jax.Sh...  0.99 us

profile of v6, /device:TPU:1, one launch (start us, length us, event | category | flops | bytes accessed | tf_op | source)
XLA Modules:
  0.0 15.9 jit_solution(4347592681158853559)
XLA Ops:
  0.6 14.2 %shard_map.68 = (f32[1024,128]{1,0:T(8,128)S(1)}, f32[8,8,16,128]{3,2,1,0:T(8,128)S(1)}, f32[8,8,16,128]{3,2,1,0:T(8,128)S(1)}, f32[8,8,16,128]{3,2,1,0:T(8,128)...) custom-call(f32[1024,128]{1,0:T(8,128)} %bitcast.6, f32[8,8,16,128]{3,2,1,0:T(8,128)} %bitcast.7, ...), custom_call_target="tpu_custom_call" | custom-call | tf_op jit(solution)/shard_map/pallas_call | solution.py:487
  14.9 1.0 %shard_map.69 = (f32[1024,128]{1,0:T(8,128)}, f32[8,8,16,128]{3,2,1,0:T(8,128)}) custom-call(f32[1024,128]{1,0:T(8,128)S(1)} %get-tuple-element.10.res, f32[8,8,16,128]{3,2,1,0:T(8,128)S(1)} %get-tuple-element.11.weight, f32[8,8,16,128]{3,2,1,0:T(8,128)S(1)} %get-tuple-element.12.coef_t, f32[8,8,16,128]{3,2,1,0:T(8,128)S(1)} %get-tuple-element.13.coef_u, ...), custom_call_target="tpu_custom_call" | custom-call | tf_op jit(solution)/shard_map/pallas_call | solution.py:515

commit v7 on v6

--- a/solution.py
+++ b/solution.py
@@ -166,7 +166,7 @@
     chip_send[...] = dense
 
     pl.semaphore_wait(barrier, sum(met.astype(jnp.int32) for met in greets + list(has[2:])))
-    for side in (2, 3, 4, 5, 0, 1):
+    for side in (1, 0, 2, 3, 4, 5):
         halo_start(side)
 
 

time: 16 us -> 16 us (level)
  no operation moved by 1% of the time
where the time goes in v7:
time: 16 us; the launch traced here: 15.9 us
  Pallas kernels  15.2 us (95%)
  between operations  0.64 us (4%)
    pallas_call x1, Pallas kernels, shards(): pl.pallas_call(functools.partial(kernel, *counts), out_shape=(rows, whole...  14.2 us
    pallas_call x1, Pallas kernels, shards(): pl.pallas_call(finish, out_shape=(jax.ShapeDtypeStruct(flat, F32), jax.Sh...  0.99 us

profile of v7, /device:TPU:1, one launch (start us, length us, event | category | flops | bytes accessed | tf_op | source)
XLA Modules:
  0.0 15.9 jit_solution(8461662170356532339)
XLA Ops:
  0.6 14.2 %shard_map.68 = (f32[1024,128]{1,0:T(8,128)S(1)}, f32[8,8,16,128]{3,2,1,0:T(8,128)S(1)}, f32[8,8,16,128]{3,2,1,0:T(8,128)S(1)}, f32[8,8,16,128]{3,2,1,0:T(8,128)...) custom-call(f32[1024,128]{1,0:T(8,128)} %bitcast.6, f32[8,8,16,128]{3,2,1,0:T(8,128)} %bitcast.7, ...), custom_call_target="tpu_custom_call" | custom-call | tf_op jit(solution)/shard_map/pallas_call | solution.py:487
  14.9 1.0 %shard_map.69 = (f32[1024,128]{1,0:T(8,128)}, f32[8,8,16,128]{3,2,1,0:T(8,128)}) custom-call(f32[1024,128]{1,0:T(8,128)S(1)} %get-tuple-element.10.res, f32[8,8,16,128]{3,2,1,0:T(8,128)S(1)} %get-tuple-element.11.weight, f32[8,8,16,128]{3,2,1,0:T(8,128)S(1)} %get-tuple-element.12.coef_t, f32[8,8,16,128]{3,2,1,0:T(8,128)S(1)} %get-tuple-element.13.coef_u, ...), custom_call_target="tpu_custom_call" | custom-call | tf_op jit(solution)/shard_map/pallas_call | solution.py:515

commit v8 on v6

--- a/solution.py
+++ b/solution.py
@@ -453,7 +453,7 @@
 
 
 def finish(res, weight, coef_t, coef_u, coef_q, run_ends, res_hbm, heat_hbm, heat, sem):
-    copies = [pltpu.make_async_copy(res, res_hbm, sem.at[2])]
+    copies = [pltpu.make_async_copy(res, res_hbm, sem.at[4])]
     copies[0].start()
     xa, x = run_ends[0], run_ends[1]
     for i in range(STEPS - 1, -1, -1):
@@ -462,10 +462,10 @@
         elif i < STEPS - 1:
             x = coef_q[:, i] + coef_u[:, i] * xa + coef_t[:, i] * x
         heat[:, i] = weight[:, i] * x
-        if i % 4 == 0:
-            part = pl.ds(i, 4)
+        if i % 2 == 0:
+            part = pl.ds(i, 2)
             copies.append(
-                pltpu.make_async_copy(heat.at[:, part], heat_hbm.at[:, part], sem.at[i // 4])
+                pltpu.make_async_copy(heat.at[:, part], heat_hbm.at[:, part], sem.at[i // 2])
             )
             copies[-1].start()
     for copy in copies:
@@ -517,7 +517,7 @@
         out_shape=(jax.ShapeDtypeStruct(flat, F32), jax.ShapeDtypeStruct(shape, F32)),
         in_specs=[vmem_space] * 6,
         out_specs=(hbm_space, hbm_space),
-        scratch_shapes=[whole, dma((3,))],
+        scratch_shapes=[whole, dma((5,))],
     )(*(pltpu.with_memory_space_constraint(array, pltpu.VMEM) for array in held))
     return residual.reshape(warmth_field.shape), heat_rate.reshape(warmth_field.shape)
 

time: 16 us -> 16 us (level)
  no operation moved by 1% of the time
where the time goes in v8:
time: 16 us; the launch traced here: 15.9 us
  Pallas kernels  15.2 us (95%)
  between operations  0.64 us (4%)
    pallas_call x1, Pallas kernels, shards(): pl.pallas_call(functools.partial(kernel, *counts), out_shape=(rows, whole...  14.2 us
    pallas_call x1, Pallas kernels, shards(): pl.pallas_call(finish, out_shape=(jax.ShapeDtypeStruct(flat, F32), jax.Sh...  1 us

profile of v8, /device:TPU:1, one launch (start us, length us, event | category | flops | bytes accessed | tf_op | source)
XLA Modules:
  0.0 15.9 jit_solution(11821410992062345866)
XLA Ops:
  0.6 14.2 %shard_map.68 = (f32[1024,128]{1,0:T(8,128)S(1)}, f32[8,8,16,128]{3,2,1,0:T(8,128)S(1)}, f32[8,8,16,128]{3,2,1,0:T(8,128)S(1)}, f32[8,8,16,128]{3,2,1,0:T(8,128)...) custom-call(f32[1024,128]{1,0:T(8,128)} %bitcast.6, f32[8,8,16,128]{3,2,1,0:T(8,128)} %bitcast.7, ...), custom_call_target="tpu_custom_call" | custom-call | tf_op jit(solution)/shard_map/pallas_call | solution.py:487
  14.9 1.0 %shard_map.69 = (f32[1024,128]{1,0:T(8,128)}, f32[8,8,16,128]{3,2,1,0:T(8,128)}) custom-call(f32[1024,128]{1,0:T(8,128)S(1)} %get-tuple-element.10.res, f32[8,8,16,128]{3,2,1,0:T(8,128)S(1)} %get-tuple-element.11.weight, f32[8,8,16,128]{3,2,1,0:T(8,128)S(1)} %get-tuple-element.12.coef_t, f32[8,8,16,128]{3,2,1,0:T(8,128)S(1)} %get-tuple-element.13.coef_u, ...), custom_call_target="tpu_custom_call" | custom-call | tf_op jit(solution)/shard_map/pallas_call | solution.py:515
